TPU v7x, 256 devices: a whole 4x4x8 slice. The times are simulated.
256 devices in a mesh: grp: 8 (over z), sfc: 32 (over y, x, core).
Axes of the slice: x: 4, y: 4, z: 8, core: 2. Of those that a mesh axis runs over, the one named last changes fastest.
Arguments:
- old_coef: bfloat16 [64, 64, 32768], P(None, None, ('grp', 'sfc')), may hold values from 0.5 to 8
- refine_flags: int32 [32768], P(('grp', 'sfc')), may hold values from 0 to 1, as said below
- counts: int32 [256], P(('grp', 'sfc')), may hold values from 1 to 128, as said below
- right_side: float32 [64, 64, 32768], P(None, None, ('grp', 'sfc')), may hold values from -6 to 6
- nbr_first: int32 [4, 32768], P(None, ('grp', 'sfc')), may hold values from 0 to 32767, as said below
- nbr_second: int32 [4, 32768], P(None, ('grp', 'sfc')), may hold values from 0 to 32767, as said below
- face_kind: int32 [4, 32768], P(None, ('grp', 'sfc')), may hold values from 0 to 4
Outputs:
- solution: float32 [64, 64, 32768], P(None, None, ('grp', 'sfc'))
- residual: float32 [64, 64, 32768], P(None, None, ('grp', 'sfc'))
Inputs may be any that keep to these rules, and one draw needn't show every extreme that they name: `refine_flags`: 0 or 1; 0 in the slots of a device at or past its count. The number of new leaves, count + 3 * (flags) of a device, summed over devices 0 .. e (the flattened index over grp then sfc) is (e + 1) * 128 + drift_e with 0 <= drift_e <= 63, drift 0 at the last device and 63 at some device. `counts`: old leaves fill the first slots of a device. `nbr_first`: global new leaf index; the device owning it sits at the same grp and sfc index as the leaf's owner or differs by one in exactly one of the two. Equal to the leaf itself for face_kind 0. `nbr_second`: as nbr_first, and equal to it unless face_kind is 4; then on the same device as nbr_first.
All inputs are finite; a program needn't handle non-finite values.
Results may differ from a plain program's by a relative error of at most 0.0003.
Values may be sent and summed in bfloat16 or wider, within the bound.
No kernel may reach another device: no remote copies, remote signals or barrier semaphores. Data moves between devices by JAX's collectives and lax.ppermute only.
A program may use at most 128 MiB of HBM per device.

v0:
```python
import jax
import jax.numpy as jnp
from jax import lax
from jax.sharding import PartitionSpec as P

LOWER_BOUND = 0.3
UPPER_BOUND = 1.9


def prefix(part, axis, combine, identity):
    place = lax.axis_index(axis)
    gathered = lax.all_gather(part, axis)
    state = jnp.zeros_like(part) + jnp.asarray(identity, part.dtype)

    def one(lap, state):
        return combine(state, lax.dynamic_index_in_dim(gathered, lap, 0, False))

    return lax.fori_loop(0, place, one, state)


def shifted(value, axis, steps):
    count = lax.axis_size(axis)
    initial, last = (max(0, -steps), min(count, count - steps))
    return lax.ppermute(value, axis, [(source, source + steps) for source in range(initial, last)])


def extended(cells, sides, width):
    for axis, dim in sides:
        count = lax.axis_size(axis)
        ends = count - 1
        head = lax.slice_in_dim(cells, 0, width, axis=dim)
        tail = lax.slice_in_dim(cells, cells.shape[dim] - width, cells.shape[dim], axis=dim)
        cells = jnp.concatenate(
            [
                lax.ppermute(tail, axis, [(i, (i + 1) % count) for i in range(ends)]),
                cells,
                lax.ppermute(head, axis, [((i + 1) % count, i) for i in range(ends)]),
            ],
            axis=dim,
        )
    return cells


def refine(coef_blocks, parent, child_index, quadrant):
    extent = coef_blocks.shape[0]
    halfway = extent // 2
    picked = jnp.take(coef_blocks, parent, axis=2)
    leaf_count = picked.shape[2]
    quarters = picked.reshape(2, halfway, 2, halfway, leaf_count)
    first_bit = child_index % 2 == 1
    second_bit = child_index // 2 == 1
    rows_picked = jnp.where(first_bit[None, None, None, :], quarters[1], quarters[0])
    chosen = jnp.where(second_bit[None, None, :], rows_picked[:, 1], rows_picked[:, 0])
    doubled = jnp.broadcast_to(
        chosen[:, None, :, None, :], (halfway, 2, halfway, 2, leaf_count)
    ).reshape(extent, extent, leaf_count)
    return jnp.where(quadrant[None, None, :], doubled, picked)


def boundary(iterate):
    return jnp.stack([iterate[0], iterate[-1], iterate[:, 0], iterate[:, -1]], axis=1)


def facing_index():
    face_ids = jnp.arange(4, dtype=jnp.int32)[:, None]
    return face_ids + 1 - 2 * (face_ids % 2)


def hang(leading, second, face_kind):
    halfway = leading.shape[0] // 2
    lower_half = jnp.repeat(leading[:halfway], 2, axis=0)
    upper_half = jnp.repeat(leading[halfway:], 2, axis=0)
    coarse = (
        jnp.concatenate([leading[0::2] + leading[1::2], second[0::2] + second[1::2]], axis=0) * 0.5
    )
    return jnp.where(
        face_kind == 1,
        leading,
        jnp.where(
            face_kind == 2,
            lower_half,
            jnp.where(
                face_kind == 3,
                upper_half,
                jnp.where(face_kind == 4, coarse, jnp.zeros_like(leading)),
            ),
        ),
    )


def apply_operator(iterate, diagonal, ghost):
    upward = jnp.concatenate([ghost[:, 0][None], iterate[:-1]], axis=0)
    downward = jnp.concatenate([iterate[1:], ghost[:, 1][None]], axis=0)
    leftward = jnp.concatenate([ghost[:, 2][:, None], iterate[:, :-1]], axis=1)
    rightward = jnp.concatenate([iterate[:, 1:], ghost[:, 3][:, None]], axis=1)
    return diagonal * iterate - (upward + downward + leftward + rightward)


def chebyshev(right_side, diagonal, ghost_of):
    middle = (UPPER_BOUND + LOWER_BOUND) / 2.0
    radius = (UPPER_BOUND - LOWER_BOUND) / 2.0
    spread_ratio = middle / radius
    factor = 1.0 / spread_ratio
    update = right_side / diagonal / middle
    solution = jnp.zeros_like(right_side)
    residual = right_side
    for iteration in range(3):
        solution = solution + update
        residual = right_side - apply_operator(solution, diagonal, ghost_of(boundary(solution)))
        if iteration < 2:
            factor_next = 1.0 / (2.0 * spread_ratio - factor)
            update = factor_next * factor * update + 2.0 * factor_next / radius * (
                residual / diagonal
            )
            factor = factor_next
    return (solution, residual)


def add_counts(earlier, later):
    return earlier + later


def build_leaves(window_coef, window_weight, inclusive, targets):
    starts = inclusive - window_weight
    parent = jnp.clip(jnp.searchsorted(inclusive, targets, side="right"), 0, inclusive.shape[0] - 1)
    child_index = targets - jnp.take(starts, parent)
    quadrant = jnp.take(window_weight, parent) == 4
    created = refine(window_coef, parent, child_index, quadrant)
    inside = (targets >= starts[0]) & (targets < inclusive[-1])
    return jnp.where(inside[None, None, :], created, jnp.zeros_like(created))


def body(old_coef, refine_flags, counts, right_side, nbr_first, nbr_second, face_kind):
    old_slots = refine_flags.shape[0]
    new_slots = right_side.shape[2]
    sfc_count = lax.axis_size("sfc")
    here_grp = lax.axis_index("grp")
    here_sfc = lax.axis_index("sfc")
    position = here_grp * sfc_count + here_sfc
    slot_index = jnp.arange(old_slots, dtype=jnp.int32)
    weight = jnp.where(slot_index < counts[0], 1 + 3 * refine_flags, 0)
    produced = jnp.sum(weight).reshape(1)
    offset = prefix(produced, ("grp", "sfc"), add_counts, jnp.zeros((1,), jnp.int32))[0]
    first_leaf = position * new_slots
    prev_coef, prev_weight = shifted((old_coef, weight.astype(jnp.bfloat16)), ("grp", "sfc"), 1)
    prev_weight = prev_weight.astype(jnp.int32)
    window_weight = jnp.concatenate([prev_weight, weight])
    inclusive = (offset - jnp.sum(prev_weight) + jnp.cumsum(window_weight)).astype(jnp.int32)
    targets = first_leaf + jnp.arange(new_slots, dtype=jnp.int32)
    coefficient = build_leaves(
        jnp.concatenate([prev_coef, old_coef], axis=2), window_weight, inclusive, targets
    )
    diagonal = 4.0 + coefficient.astype(jnp.float32)
    facing = facing_index()

    def column_of(neighbour):
        owner_dev = neighbour // new_slots
        owner_grp = owner_dev // sfc_count
        owner_sfc = owner_dev % sfc_count
        source_slot = jnp.where(
            owner_grp < here_grp,
            1,
            jnp.where(
                owner_grp > here_grp,
                2,
                jnp.where(owner_sfc < here_sfc, 3, jnp.where(owner_sfc > here_sfc, 4, 0)),
            ),
        )
        return ((source_slot * 4 + facing) * new_slots + neighbour % new_slots).reshape(-1)

    index_first = column_of(nbr_first)
    index_second = column_of(nbr_second)

    def ghost_of(face_values):
        extent = face_values.shape[0]
        beside_all = extended(face_values[:, None, None], (("grp", 1), ("sfc", 2)), 1)
        candidates = jnp.stack(
            [
                beside_all[:, 1, 1],
                beside_all[:, 0, 1],
                beside_all[:, 2, 1],
                beside_all[:, 1, 0],
                beside_all[:, 1, 2],
            ],
            axis=1,
        ).reshape(extent, -1)
        leading = jnp.take(candidates, index_first, axis=1).reshape(face_values.shape)
        second = jnp.take(candidates, index_second, axis=1).reshape(face_values.shape)
        return hang(leading, second, face_kind)

    return chebyshev(right_side, diagonal, ghost_of)


def solution(mesh):
    placed = (
        P(None, None, ("grp", "sfc")),
        P(("grp", "sfc")),
        P(("grp", "sfc")),
        P(None, None, ("grp", "sfc")),
        P(None, ("grp", "sfc")),
        P(None, ("grp", "sfc")),
        P(None, ("grp", "sfc")),
    )
    return jax.shard_map(
        body,
        mesh=mesh,
        in_specs=placed,
        out_specs=(P(None, None, ("grp", "sfc")), P(None, None, ("grp", "sfc"))),
        check_vma=False,
    )
```

profile of v0, /device:TPU:216, one launch (start us, length us, event | category | flops | bytes accessed | tf_op | source)
XLA Modules:
  0.0 747.9 jit_solution(11681454179943906785)
XLA Ops:
  4.5 3.5 collective-permute-start.1
  8.8 78.2 %all-reduce = s32[256]{0:T(256)S(1)} all-reduce(s32[256]{0:T(256)S(1)} %dynamic-update-slice), channel_id=1, replica_groups=mesh['grp'=8,'sfc'=32] {'grp','sfc'}, use_global_device_ids=true, to_apply=%add | all-reduce | flops 256 | bytes 2048
  87.0 277.7 %while.34 = (s32[]{:T(128)}, s32[1]{0:T(128)}, s32[]{:T(128)}, s32[256,1]{0,1:T(1,128)S(1)}, s32[]{:T(128)}, /*index=5*/s32[]{:T(128)}, s32[]{:T(128)}) while((s32[]{:T(128)}, s32[1]{0:T(128)}, s32[]{:T(128)}, s32[256,1]{0,1:T(1,128)S(1)}, s32[]{:T(128)}, /*index=5*/s32[]{:T(128)}, s32[]{:T(128)}) %tuple.104), condition=%wide.region_2.3_spmd, body=%wide.region_1.2_spmd.sunk | while | flops 6 | bytes 143 | solution.py:18
  366.3 3.9 copy.222
  370.1 5.6 copy.226
  377.7 12.0 %while.35 = (s32[]{:T(128)}, u32[128]{0:T(128)S(1)}, u32[128]{0:T(128)S(1)}, s32[256]{0:T(256)S(1)}, s32[]{:T(128)}, /*index=5*/s32[]{:T(128)}, s32[]{:T(128)}, s32[]{}) while((s32[]{:T(128)}, u32[128]{0:T(128)S(1)}, u32[128]{0:T(128)S(1)}, s32[256]{0:T(256)S(1)}, s32[]{:T(128)}, /*index=5*/s32[]{:T(128)}, s32[]{:T(128)}, ...), condition=%wide.region_7.8_spmd.clone, body=%wide.region_6.7_spmd.clone.sunk | while | flops 2820 | bytes 10352 | solution.py:125
  394.7 3.7 copy.221
  398.4 4.4 pad_maximum_fusion
  402.8 3.1 gather_fusion.1
  407.6 2.2 copy.224
  412.1 3.7 copy.225
  415.8 4.7 fusion.24
  420.6 4.7 fusion.75
  425.5 3.8 copy.229
  429.2 3.7 copy.230
  433.0 2.2 collective-permute-start.3
  435.2 43.8 %collective-permute-start.2 = (f32[64,1,1,4,128]{4,0,3,2,1:T(8,128)S(1)}, f32[64,1,1,4,128]{4,0,3,2,1:T(8,128)S(1)}, u32[]{:S(2)}, u32[]{:S(2)}) collective-permute-start(f32[64,1,1,4,128]{4,0,3,2,1:T(8,128)S(1)} %fusion.46), channel_id=1, source_target_pairs={{0,32},{32,64},{64,96},{96,128},{128,160},{160,192},{192,224},{1,3... | collective-permute-start | bytes 393224 | tf_op jit(solution)/shard_map/ppermute | solution.py:35
  479.0 8.7 %fusion.72 = (f32[63,64,128]{1,0,2:T(8,128)}, f32[63,64,128]{1,0,2:T(8,128)}) fusion(f32[64,64,128]{1,0,2:T(8,128)} %copy-done.3), kind=kLoop, calls=%fused_computation.186 | loop fusion | bytes 8257536 | tf_op jit(solution)/shard_map/slice | solution.py:92
  487.6 4.8 fusion.73
  493.1 1.9 collective-permute-start.5
  495.0 2.7 collective-permute-start.4
  499.1 7.1 collective-permute-done.4
  509.1 2.1 gather_fusion.5
  512.9 3.8 slice.245
  516.7 3.9 slice.246
  524.5 2.3 slice.243
  526.8 2.4 slice.244
  532.4 4.5 copy.244
  536.9 4.4 copy.243
  541.4 13.8 %fusion.61 = (f32[64,64,128]{1,0,2:T(8,128)S(1)}, f32[64,64,128]{1,0,2:T(8,128)}) fusion(f32[64,64,128]{1,0,2:T(8,128)} %copy.226, bf16[64,64,128]{1,0,2:T(8,128)(2,1)S(1)} %get-tuple-element.148, f32[64,1,128]{1,0,2:T(8,128)} %copy.244, f32[64,63,128]{1,0,2:T(8,128)} %get-tuple-element.178, f32[64,63,128]{1,0,2:T(8,128)} %get-tuple-element.177, ...), kind=kLoop, calls=%fused_computation.176 | loop fusion | flops 9961472 | bytes 15728640 | tf_op jit(solution)/shard_map/add | solution.py:108
  555.3 4.8 fusion.71
  560.2 3.9 copy.248
  564.2 3.7 copy.249
  567.9 2.2 collective-permute-start.7
  570.1 3.9 collective-permute-start.6
  574.1 8.7 %fusion.69 = (f32[63,64,128]{1,0,2:T(8,128)}, f32[63,64,128]{1,0,2:T(8,128)}) fusion(f32[64,64,128]{1,0,2:T(8,128)} %copy-done.1), kind=kLoop, calls=%fused_computation.183 | loop fusion | bytes 8257536 | tf_op jit(solution)/shard_map/slice | solution.py:93
  582.7 4.7 fusion.68
  590.0 2.4 collective-permute-start.8
  593.8 7.5 collective-permute-done.8
  608.5 2.9 slice.267
  611.4 2.4 slice.268
  616.1 2.3 slice.265
  618.4 2.4 slice.266
  623.6 4.5 copy.263
  628.1 4.5 copy.262
  632.6 13.1 %fusion.18 = f32[64,64,128]{1,0,2:T(8,128)S(1)} fusion(f32[64,64,128]{1,0,2:T(8,128)} %copy.226, f32[63,64,128]{1,0,2:T(8,128)} %get-tuple-element.170, f32[1,64,128]{1,0,2:T(1,128)S(1)} %copy.260, f32[1,64,128]{1,0,2:T(1,128)S(1)} %copy.261, f32[63,64,128]{1,0,2:T(8,128)} %get-tuple-element.169, f32[64,63,128]{1,0,2:T(8,128)} %get-tuple-element.168, ...), kind=kLoop, calls=%fused_computation.36 | loop fusion | flops 10485760 | bytes 15728640 | tf_op jit(solution)/shard_map/add | solution.py:108
  645.8 4.8 fusion.64
  650.6 4.9 fusion.67
  655.6 3.8 copy.267
  659.4 3.7 copy.268
  663.1 1.9 collective-permute-start.11
  665.1 3.9 collective-permute-start.10
  669.0 8.8 %fusion.65 = (f32[63,64,128]{1,0,2:T(8,128)}, f32[63,64,128]{1,0,2:T(8,128)}) fusion(f32[64,64,128]{1,0,2:T(8,128)} %copy-done), kind=kLoop, calls=%fused_computation.179 | loop fusion | bytes 8257536 | tf_op jit(solution)/shard_map/slice | solution.py:93
  677.8 4.8 copy.284
  685.2 2.4 collective-permute-start.12
  688.9 7.5 collective-permute-done.12
  703.8 2.9 slice.289
  706.8 2.4 slice.290
  711.5 2.3 slice.287
  713.8 2.4 slice.288
  719.0 4.5 copy.282
  723.5 4.5 copy.281
  727.9 14.7 %fusion.22 = f32[64,64,128]{1,0,2:T(8,128)} fusion(f32[64,64,128]{1,0,2:T(8,128)} %copy.226, f32[63,64,128]{1,0,2:T(8,128)} %get-tuple-element.162, f32[1,64,128]{1,0,2:T(1,128)S(1)} %copy.279, f32[1,64,128]{1,0,2:T(1,128)S(1)} %copy.280, f32[63,64,128]{1,0,2:T(8,128)} %get-tuple-element.161, f32[64,63,128]{1,0,2:T(8,128)} %get-tuple-element.160, ...), kind=kLoop, calls=%fused_computation.41 | loop fusion | flops 6291456 | bytes 15728640 | tf_op jit(solution)/shard_map/sub | solution.py:109
  742.7 4.8 copy.285
  (425 shorter events, 212.3 us)
Async XLA Ops:
  2.6 373.2 %collective-permute-start = (bf16[128]{0:T(256)(128)(2,1)S(1)}, bf16[128]{0:T(256)(128)(2,1)S(1)}, u32[]{:S(2)}, u32[]{:S(2)}) collective-permute-start(bf16[128]{0:T(256)(128)(2,1)S(1)} %convert_element_type.19), channel_id=1, source_target_pairs={{0,1},{1,2},{2,3},{3,4},{4,5},{5,6},{6,7},{7,8},{8,9},{9,10},{10,1... | collective-permute-start | bytes 776 | tf_op jit(solution)/shard_map/ppermute | solution.py:24
  4.5 390.2 %collective-permute-start.1 = (bf16[64,64,128]{2,1,0:T(8,128)(2,1)}, bf16[64,64,128]{2,1,0:T(8,128)(2,1)S(1)}, u32[]{:S(2)}, u32[]{:S(2)}) collective-permute-start(bf16[64,64,128]{2,1,0:T(8,128)(2,1)} %param.15), channel_id=1, source_target_pairs={{0,1},{1,2},{2,3},{3,4},{4,5},{5,6},{6,7},{7,8},{8,9},{9,10},{10,1... | collective-permute-start | bytes 3145736 | tf_op jit(solution)/shard_map/ppermute | solution.py:24
  365.5 166.7 %copy-start.6 = (pred[4,128]{1,0:T(4,128)(4,1)}, pred[4,128]{1,0:T(4,128)(4,1)S(1)}, u32[]{:S(2)}) copy-start(pred[4,128]{1,0:T(4,128)(4,1)S(1)} %get-tuple-element.204) | copy-start | bytes 1540
  365.5 166.7 %copy-start.8 = (pred[4,128]{1,0:T(4,128)(4,1)}, pred[4,128]{1,0:T(4,128)(4,1)S(1)}, u32[]{:S(2)}) copy-start(pred[4,128]{1,0:T(4,128)(4,1)S(1)} %get-tuple-element.205) | copy-start | bytes 1540
  365.5 166.7 %copy-start.10 = (pred[4,128]{1,0:T(4,128)(4,1)}, pred[4,128]{1,0:T(4,128)(4,1)S(1)}, u32[]{:S(2)}) copy-start(pred[4,128]{1,0:T(4,128)(4,1)S(1)} %get-tuple-element.206) | copy-start | bytes 1540
  366.2 241.1 %copy-start.11 = (pred[512]{0:T(512)(128)(4,1)}, pred[512]{0:T(512)(128)(4,1)S(1)}, u32[]{:S(2)}) copy-start(pred[512]{0:T(512)(128)(4,1)S(1)} %get-tuple-element.143) | copy-start | bytes 1540
  406.0 1.7 copy-start.5
  420.5 4.8 copy-start.3
  433.0 54.7 %copy-start.4 = (f32[64,64,128]{1,0,2:T(8,128)S(1)}, f32[64,64,128]{1,0,2:T(8,128)}, u32[]{:S(2)}) copy-start(f32[64,64,128]{1,0,2:T(8,128)} %copy-done.3) | copy-start | bytes 6291460
  433.0 60.1 %collective-permute-start.3 = (f32[64,1,1,4,128]{4,0,3,2,1:T(8,128)S(1)}, f32[64,1,1,4,128]{4,0,3,2,1:T(8,128)S(1)}, u32[]{:S(2)}, u32[]{:S(2)}) collective-permute-start(f32[64,1,1,4,128]{4,0,3,2,1:T(8,128)S(1)} %fusion.46), channel_id=1, source_target_pairs={{32,0},{64,32},{96,64},{128,96},{160,128},{192,160},{224,192},{33,... | collective-permute-start | bytes 393224 | tf_op jit(solution)/shard_map/ppermute | solution.py:37
  435.2 57.9 %collective-permute-start.2 = (f32[64,1,1,4,128]{4,0,3,2,1:T(8,128)S(1)}, f32[64,1,1,4,128]{4,0,3,2,1:T(8,128)S(1)}, u32[]{:S(2)}, u32[]{:S(2)}) collective-permute-start(f32[64,1,1,4,128]{4,0,3,2,1:T(8,128)S(1)} %fusion.46), channel_id=1, source_target_pairs={{0,32},{32,64},{64,96},{96,128},{128,160},{160,192},{192,224},{1,3... | collective-permute-start | bytes 393224 | tf_op jit(solution)/shard_map/ppermute | solution.py:35
  493.1 13.8 %collective-permute-start.5 = (f32[64,3,1,4,128]{4,0,3,2,1:T(8,128)S(1)}, f32[64,3,1,4,128]{4,0,3,2,1:T(8,128)S(1)}, u32[]{:S(2)}, u32[]{:S(2)}) collective-permute-start(f32[64,3,1,4,128]{4,0,3,2,1:T(8,128)S(1)} %pad_maximum_fusion.1), channel_id=1, source_target_pairs={{1,0},{2,1},{3,2},{4,3},{5,4},{6,5},{7,6},{8,7},{9,8},{10,9},{11,1... | collective-permute-start | bytes 1179656 | tf_op jit(solution)/shard_map/ppermute | solution.py:37
  495.0 11.2 %collective-permute-start.4 = (f32[64,3,1,4,128]{4,0,3,2,1:T(8,128)S(1)}, f32[64,3,1,4,128]{4,0,3,2,1:T(8,128)S(1)}, u32[]{:S(2)}, u32[]{:S(2)}) collective-permute-start(f32[64,3,1,4,128]{4,0,3,2,1:T(8,128)S(1)} %pad_maximum_fusion.1), channel_id=1, source_target_pairs={{0,1},{1,2},{2,3},{3,4},{4,5},{5,6},{6,7},{7,8},{8,9},{9,10},{10,1... | collective-permute-start | bytes 1179656 | tf_op jit(solution)/shard_map/ppermute | solution.py:35
  555.2 4.9 copy-start.1
  567.9 14.8 %copy-start.2 = (f32[64,64,128]{1,0,2:T(8,128)S(1)}, f32[64,64,128]{1,0,2:T(8,128)}, u32[]{:S(2)}) copy-start(f32[64,64,128]{1,0,2:T(8,128)} %copy-done.1) | copy-start | bytes 6291460
  567.9 20.1 %collective-permute-start.7 = (f32[64,1,1,4,128]{4,0,3,2,1:T(8,128)S(1)}, f32[64,1,1,4,128]{4,0,3,2,1:T(8,128)S(1)}, u32[]{:S(2)}, u32[]{:S(2)}) collective-permute-start(f32[64,1,1,4,128]{4,0,3,2,1:T(8,128)S(1)} %fusion.45), channel_id=1, source_target_pairs={{32,0},{64,32},{96,64},{128,96},{160,128},{192,160},{224,192},{33,... | collective-permute-start | bytes 393224 | tf_op jit(solution)/shard_map/ppermute | solution.py:37
  570.1 18.0 %collective-permute-start.6 = (f32[64,1,1,4,128]{4,0,3,2,1:T(8,128)S(1)}, f32[64,1,1,4,128]{4,0,3,2,1:T(8,128)S(1)}, u32[]{:S(2)}, u32[]{:S(2)}) collective-permute-start(f32[64,1,1,4,128]{4,0,3,2,1:T(8,128)S(1)} %fusion.45), channel_id=1, source_target_pairs={{0,32},{32,64},{64,96},{96,128},{128,160},{160,192},{192,224},{1,3... | collective-permute-start | bytes 393224 | tf_op jit(solution)/shard_map/ppermute | solution.py:35
  588.1 13.8 %collective-permute-start.9 = (f32[64,3,1,4,128]{4,0,3,2,1:T(8,128)S(1)}, f32[64,3,1,4,128]{4,0,3,2,1:T(8,128)S(1)}, u32[]{:S(2)}, u32[]{:S(2)}) collective-permute-start(f32[64,3,1,4,128]{4,0,3,2,1:T(8,128)S(1)} %pad_maximum_fusion.2), channel_id=1, source_target_pairs={{1,0},{2,1},{3,2},{4,3},{5,4},{6,5},{7,6},{8,7},{9,8},{10,9},{11,1... | collective-permute-start | bytes 1179656 | tf_op jit(solution)/shard_map/ppermute | solution.py:37
  590.0 11.2 %collective-permute-start.8 = (f32[64,3,1,4,128]{4,0,3,2,1:T(8,128)S(1)}, f32[64,3,1,4,128]{4,0,3,2,1:T(8,128)S(1)}, u32[]{:S(2)}, u32[]{:S(2)}) collective-permute-start(f32[64,3,1,4,128]{4,0,3,2,1:T(8,128)S(1)} %pad_maximum_fusion.2), channel_id=1, source_target_pairs={{0,1},{1,2},{2,3},{3,4},{4,5},{5,6},{6,7},{7,8},{8,9},{9,10},{10,1... | collective-permute-start | bytes 1179656 | tf_op jit(solution)/shard_map/ppermute | solution.py:35
  645.7 4.9 copy-start
  663.1 20.1 %collective-permute-start.11 = (f32[64,1,1,4,128]{4,0,3,2,1:T(8,128)S(1)}, f32[64,1,1,4,128]{4,0,3,2,1:T(8,128)S(1)}, u32[]{:S(2)}, u32[]{:S(2)}) collective-permute-start(f32[64,1,1,4,128]{4,0,3,2,1:T(8,128)S(1)} %fusion.44), channel_id=1, source_target_pairs={{32,0},{64,32},{96,64},{128,96},{160,128},{192,160},{224,192},{33,... | collective-permute-start | bytes 393224 | tf_op jit(solution)/shard_map/ppermute | solution.py:37
  665.1 18.1 %collective-permute-start.10 = (f32[64,1,1,4,128]{4,0,3,2,1:T(8,128)S(1)}, f32[64,1,1,4,128]{4,0,3,2,1:T(8,128)S(1)}, u32[]{:S(2)}, u32[]{:S(2)}) collective-permute-start(f32[64,1,1,4,128]{4,0,3,2,1:T(8,128)S(1)} %fusion.44), channel_id=1, source_target_pairs={{0,32},{32,64},{64,96},{96,128},{128,160},{160,192},{192,224},{1,3... | collective-permute-start | bytes 393224 | tf_op jit(solution)/shard_map/ppermute | solution.py:35
  682.5 20.2 %copy-start.12 = (pred[512]{0:T(512)(128)(4,1)S(1)}, pred[512]{0:T(512)(128)(4,1)}, u32[]{:S(2)}) copy-start(pred[512]{0:T(512)(128)(4,1)} %copy-done.11) | copy-start | bytes 1540
  683.2 13.8 %collective-permute-start.13 = (f32[64,3,1,4,128]{4,0,3,2,1:T(8,128)S(1)}, f32[64,3,1,4,128]{4,0,3,2,1:T(8,128)S(1)}, u32[]{:S(2)}, u32[]{:S(2)}) collective-permute-start(f32[64,3,1,4,128]{4,0,3,2,1:T(8,128)S(1)} %pad_maximum_fusion.3), channel_id=1, source_target_pairs={{1,0},{2,1},{3,2},{4,3},{5,4},{6,5},{7,6},{8,7},{9,8},{10,9},{11,1... | collective-permute-start | bytes 1179656 | tf_op jit(solution)/shard_map/ppermute | solution.py:37
  685.2 11.2 %collective-permute-start.12 = (f32[64,3,1,4,128]{4,0,3,2,1:T(8,128)S(1)}, f32[64,3,1,4,128]{4,0,3,2,1:T(8,128)S(1)}, u32[]{:S(2)}, u32[]{:S(2)}) collective-permute-start(f32[64,3,1,4,128]{4,0,3,2,1:T(8,128)S(1)} %pad_maximum_fusion.3), channel_id=1, source_target_pairs={{0,1},{1,2},{2,3},{3,4},{4,5},{5,6},{6,7},{7,8},{8,9},{9,10},{10,1... | collective-permute-start | bytes 1179656 | tf_op jit(solution)/shard_map/ppermute | solution.py:35
  702.7 15.4 %copy-start.7 = (pred[4,128]{1,0:T(4,128)(4,1)S(1)}, pred[4,128]{1,0:T(4,128)(4,1)}, u32[]{:S(2)}) copy-start(pred[4,128]{1,0:T(4,128)(4,1)} %copy-done.6) | copy-start | bytes 1540
  702.7 15.4 %copy-start.9 = (pred[4,128]{1,0:T(4,128)(4,1)S(1)}, pred[4,128]{1,0:T(4,128)(4,1)}, u32[]{:S(2)}) copy-start(pred[4,128]{1,0:T(4,128)(4,1)} %copy-done.8) | copy-start | bytes 1540
where the time goes:
time: 760 us; the launch traced here: 748 us
  local copies, waits for them, and re-layouts  357 us (47%)
  loops' own time  140 us (18%)
  blocking collectives  78.2 us (10%)
  starting transfers between devices  76.7 us (10%)
  other arithmetic  70.6 us (9%)
  waiting for transfers between devices  22.1 us (3%)
    another operation x1, loops' own time, prefix(): return lax.fori_loop(0, place, one, state)  140 us
    dynamic_slice x216, local copies, waits for them, and re-layouts, one(): return combine(state, lax.dynamic_index_in_dim(gathered, lap, 0, False))  138 us
    unnamed x1, blocking collectives  78.2 us
    ppermute x6, starting transfers between devices, extended(): lax.ppermute(tail, axis, [(i, (i + 1) % count) for i in range(ends)])  59.2 us
    unnamed x53, local copies, waits for them, and re-layouts  30.9 us
    add x2, other arithmetic, chebyshev(): solution = solution + update  26.9 us
    slice x6, local copies, waits for them, and re-layouts, boundary(): iterate[:, 0]  25.9 us
    slice x7, local copies, waits for them, and re-layouts, apply_operator(): rightward = jnp.concatenate([iterate[:, 1:], ghost[:, 3][:, None]], axis=1)  22.9 us
  transfers between devices with their start and end apart: 14, of which 3 were waited for; matrix products, arithmetic and copies ran while one was open for 29% of the time, Pallas kernels for 0%

commit v1 on v0

v1 whole, which is shorter than its diff:
```python
import functools

import jax
import jax.numpy as jnp
from jax import lax
from jax.experimental import pallas as pl
from jax.experimental.pallas import tpu as pltpu
from jax.sharding import PartitionSpec as P

LOWER_BOUND = 0.3
UPPER_BOUND = 1.9
B = 64
ROWS = B * B
LANES = 128
AXES = ("grp", "sfc")

THETA = (UPPER_BOUND + LOWER_BOUND) / 2.0
DELTA = (UPPER_BOUND - LOWER_BOUND) / 2.0
SIGMA = THETA / DELTA
RHO_0 = 1.0 / SIGMA
RHO_1 = 1.0 / (2.0 * SIGMA - RHO_0)
RHO_2 = 1.0 / (2.0 * SIGMA - RHO_1)
C_1, K_1 = RHO_1 * RHO_0, 2.0 * RHO_1 / DELTA
C_2, K_2 = RHO_2 * RHO_1, 2.0 * RHO_2 / DELTA

F32 = jnp.float32
VMEM_LIMIT = 40 * 1024 * 1024


def in_vmem(array):
    return pltpu.with_memory_space_constraint(array, pltpu.VMEM)


def call(kernel, outs, scratch, smem, operands, flops):
    specs = [pl.BlockSpec(memory_space=pltpu.SMEM)] * smem
    specs += [pl.BlockSpec(memory_space=pltpu.VMEM)] * (len(operands) - smem)
    return pl.pallas_call(
        kernel,
        out_shape=outs,
        in_specs=specs,
        out_specs=[pl.BlockSpec(memory_space=pltpu.VMEM)] * len(outs),
        scratch_shapes=scratch,
        compiler_params=pltpu.CompilerParams(vmem_limit_bytes=VMEM_LIMIT),
        cost_estimate=pl.CostEstimate(flops=flops, bytes_accessed=4 << 20, transcendentals=0),
    )(*operands[:smem], *[in_vmem(a) for a in operands[smem:]])


def vmem(rows, dtype=F32):
    return pltpu.VMEM((rows, LANES), dtype)


def kept(rows, dtype=F32):
    return pltpu.VMEM((rows, LANES), dtype)


def lane_plan(position, weights_ref):
    rows = lax.broadcasted_iota(jnp.int32, weights_ref.shape, 0)
    before = jnp.where(rows < position, weights_ref[...], 0).astype(F32)
    made = jnp.sum(jnp.sum(before, axis=0, keepdims=True), axis=1, keepdims=True)
    drift = made - (position * LANES).astype(F32)
    own = weights_ref[pl.ds(position, 1), :].astype(F32)
    prev = weights_ref[pl.ds(jnp.maximum(position - 1, 0), 1), :].astype(F32)
    prev = jnp.where(position > 0, prev, 0.0)
    window = 2 * LANES
    spread = jnp.broadcast_to(jnp.concatenate([prev, own], axis=1), (LANES, window)).astype(jnp.bfloat16)
    slot = lax.broadcasted_iota(jnp.int32, (window, window), 0)
    other = lax.broadcasted_iota(jnp.int32, (window, window), 1)
    lower = jnp.where(other <= slot, 1.0, 0.0).astype(jnp.bfloat16)
    inclusive = lax.dot_general(
        lower, spread, (((1,), (1,)), ((), ())), preferred_element_type=F32
    )
    before_own = inclusive[LANES - 1 : LANES]
    inclusive = inclusive - before_own
    target = lax.broadcasted_iota(jnp.int32, (1, LANES), 1).astype(F32) - drift
    passed = inclusive <= target
    parent = jnp.sum(jnp.where(passed, 1.0, 0.0), axis=0, keepdims=True)
    start = jnp.max(jnp.where(passed, inclusive, -before_own), axis=0, keepdims=True)
    stop = jnp.min(jnp.where(passed, 1e6, inclusive), axis=0, keepdims=True)
    child = target - start
    slot_f = lax.broadcasted_iota(jnp.int32, (window, LANES), 0).astype(F32)
    one_hot = jnp.where(slot_f == parent, 1.0, 0.0).astype(jnp.bfloat16)
    refined = (stop - start) > 2.0
    first_bit = (child == 1.0) | (child == 3.0)
    second_bit = child >= 2.0
    return one_hot, refined, first_bit, second_bit


def take_faces(field_ref, faces_ref):
    faces_ref[0:B] = field_ref[0:B]
    faces_ref[B : 2 * B] = field_ref[ROWS - B : ROWS]
    faces_ref[2 * B : 3 * B] = field_ref[pl.ds(0, B, stride=B)]
    faces_ref[3 * B : 4 * B] = field_ref[pl.ds(B - 1, B, stride=B)]


def build_kernel(position_ref, weights_ref, prev_ref, own_ref, right_ref, s_ref, inv_ref, diag_ref, faces_ref, pick_ref, dup_ref):
    one_hot, refined, first_bit, second_bit = lane_plan(position_ref[0], weights_ref)
    chunk = 512

    def pick(step, carry):
        at = pl.ds(pl.multiple_of(step * chunk, chunk), chunk)
        both = jnp.concatenate([prev_ref[at], own_ref[at]], axis=1)
        pick_ref[at] = jnp.dot(both, one_hot, preferred_element_type=F32)
        return carry

    lax.fori_loop(0, ROWS // chunk, pick, 0, unroll=2)
    half = B // 2

    def leaf(row, carry):
        low = pick_ref[pl.ds(pl.multiple_of(row * B, B), B)]
        high = pick_ref[pl.ds(pl.multiple_of((row + half) * B, B), B)]
        chosen = jnp.where(first_bit, high, low)
        chosen = jnp.where(second_bit, chosen[half:], chosen[:half])
        slot = pl.multiple_of((row % 2) * B, B)
        dup_ref[pl.ds(slot, half, stride=2)] = chosen
        dup_ref[pl.ds(slot + 1, half, stride=2)] = chosen
        doubled = dup_ref[pl.ds(slot, B)]
        for k in range(2):
            at = pl.ds(pl.multiple_of((2 * row + k) * B, B), B)
            diag = 4.0 + jnp.where(refined, doubled, pick_ref[at])
            inv = 1.0 / diag
            diag_ref[at] = diag
            inv_ref[at] = inv
            s_ref[at] = right_ref[at] * inv * (1.0 / THETA)
        return carry

    lax.fori_loop(0, half, leaf, 0, unroll=2)
    take_faces(s_ref, faces_ref)


def fill_ghosts(position_ref, sources, first_ref, second_ref, kind_ref, ghost_ref, pair_ref):
    position = position_ref[0]
    half = B // 2
    for face in range(4):
        facing = face ^ 1
        kind = kind_ref[face : face + 1]
        values = []
        for index_ref in (first_ref, second_ref):
            index = index_ref[face : face + 1]
            offset = lax.shift_right_logical(index, 7) - position
            lane = jnp.broadcast_to(index & (LANES - 1), (B, LANES))
            value = jnp.zeros((B, LANES), F32)
            for faces_ref, away in sources:
                taken = jnp.take_along_axis(
                    faces_ref[facing * B : (facing + 1) * B], lane, axis=1, mode="promise_in_bounds"
                )
                value = jnp.where(offset == away, taken, value)
            values.append(value)
        leading, second = values
        at = face * 4 * B
        pair_ref[at : at + B] = leading
        pair_ref[at + B : at + 2 * B] = second
        mean_low = (pair_ref[pl.ds(at, half, stride=2)] + pair_ref[pl.ds(at + 1, half, stride=2)]) * 0.5
        mean_high = (
            pair_ref[pl.ds(at + B, half, stride=2)] + pair_ref[pl.ds(at + B + 1, half, stride=2)]
        ) * 0.5
        for part in range(2):
            for odd in range(2):
                pair_ref[pl.ds(at + (2 + part) * B + odd, half, stride=2)] = leading[
                    part * half : (part + 1) * half
                ]
        ghost = jnp.where(kind == 4, jnp.concatenate([mean_low, mean_high], axis=0), 0.0)
        ghost = jnp.where(kind == 1, leading, ghost)
        ghost = jnp.where(kind == 2, pair_ref[at + 2 * B : at + 3 * B], ghost)
        ghost = jnp.where(kind == 3, pair_ref[at + 3 * B : at + 4 * B], ghost)
        ghost_ref[face * B : (face + 1) * B] = ghost


FACE_SLICES = (pl.ds(0, B), pl.ds(ROWS - B, B), pl.ds(0, B, stride=B), pl.ds(B - 1, B, stride=B))


def sweep(field_ref, finish):
    edge = lax.broadcasted_iota(jnp.int32, (B, LANES), 0)
    is_first, is_last = edge == 0, edge == B - 1

    def plane(index, position):
        at = pl.ds(pl.multiple_of(index * B, B), B)
        centre = field_ref[at]
        if position == 0:
            total = field_ref[pl.ds((index + 1) * B, B)]
        elif position == 2:
            total = field_ref[pl.ds((index - 1) * B, B)]
        else:
            total = field_ref[pl.ds(pl.multiple_of((index - 1) * B, B), B)]
            total = total + field_ref[pl.ds(pl.multiple_of((index + 1) * B, B), B)]
        if position == 0:
            left = pltpu.roll(centre, 1, 0)
        else:
            left = field_ref[pl.ds(index * B - 1, B)]
        if position == 2:
            right = pltpu.roll(centre, B - 1, 0)
        else:
            right = field_ref[pl.ds(index * B + 1, B)]
        total = total + jnp.where(is_first, 0.0, left) + jnp.where(is_last, 0.0, right)
        finish(at, centre, total)

    plane(0, 0)

    def step(index, carry):
        plane(index, 1)
        return carry

    lax.fori_loop(1, B - 1, step, 0, unroll=2)
    plane(B - 1, 2)


def step_kernel(scale_v, scale_u, scale_n, smem_ref, own_ref, *refs):
    received, (first_ref, second_ref, kind_ref, v_ref, u_ref, inv_ref) = refs[:4], refs[4:10]
    out_ref, faces_ref, ghost_ref, pair_ref = refs[10:]
    sources = [(own_ref, 0)] + [(r, smem_ref[1 + i]) for i, r in enumerate(received)]
    fill_ghosts(smem_ref, sources, first_ref, second_ref, kind_ref, ghost_ref, pair_ref)

    def finish(at, centre, total):
        out = scale_v * centre + scale_n * (inv_ref[at] * total)
        if scale_u is not None:
            out = out + scale_u * u_ref[at]
        out_ref[at] = out

    sweep(v_ref, finish)
    for face, at in enumerate(FACE_SLICES):
        out_ref[at] = out_ref[at] + scale_n * (inv_ref[at] * ghost_ref[face * B : (face + 1) * B])
    take_faces(out_ref, faces_ref)


def residual_kernel(smem_ref, own_ref, *refs):
    received, (first_ref, second_ref, kind_ref, v_ref, u_ref, diag_ref) = refs[:4], refs[4:10]
    out_ref, ghost_ref, pair_ref = refs[10:]
    sources = [(own_ref, 0)] + [(r, smem_ref[1 + i]) for i, r in enumerate(received)]
    fill_ghosts(smem_ref, sources, first_ref, second_ref, kind_ref, ghost_ref, pair_ref)

    def finish(at, centre, total):
        out_ref[at] = diag_ref[at] * (THETA * u_ref[at] - centre) + total

    sweep(v_ref, finish)
    for face, at in enumerate(FACE_SLICES):
        out_ref[at] = out_ref[at] + ghost_ref[face * B : (face + 1) * B]


def swap(value, axis, parity):
    count = lax.axis_size(axis)
    pairs = []
    for low in range(parity, count - 1, 2):
        pairs += [(low, low + 1), (low + 1, low)]
    return lax.ppermute(value, axis, pairs)


def exchange(faces):
    return [swap(faces, "sfc", 1), swap(faces, "grp", 1), swap(faces, "grp", 0), swap(faces, "sfc", 0)]


def body(old_coef, refine_flags, counts, right_side, nbr_first, nbr_second, face_kind):
    grp, sfc = lax.axis_index("grp"), lax.axis_index("sfc")
    n_sfc = lax.axis_size("sfc")
    devices = lax.axis_size(AXES)
    position = grp * n_sfc + sfc
    prev_coef = lax.ppermute(old_coef, AXES, [(i, i + 1) for i in range(devices - 1)])
    slots = jnp.arange(LANES, dtype=jnp.int32)
    weight = jnp.where(slots < counts[0], 1 + 3 * refine_flags, 0)
    weights = lax.all_to_all(
        jnp.broadcast_to(weight[None], (devices, LANES)), AXES, 0, 0, tiled=True
    )
    to_odd_sfc, to_odd_grp = 2 * (sfc % 2) - 1, n_sfc * (2 * (grp % 2) - 1)
    scalars = jnp.stack([position, to_odd_sfc, to_odd_grp, -to_odd_grp, -to_odd_sfc]).astype(jnp.int32)

    s1, inv, diag, faces = call(
        build_kernel,
        [kept(ROWS), kept(ROWS), kept(ROWS), kept(4 * B)],
        [vmem(ROWS), vmem(2 * B)],
        1,
        [scalars, weights, prev_coef.reshape(ROWS, LANES), old_coef.reshape(ROWS, LANES), right_side.reshape(ROWS, LANES)],
        300_000_000,
    )
    plan = [nbr_first, nbr_second, face_kind]
    scratch = [vmem(4 * B), vmem(16 * B)]
    s2, faces_2 = call(
        functools.partial(step_kernel, 1.0 + C_1 + K_1 * (THETA - 1.0), None, K_1),
        [kept(ROWS), kept(4 * B)],
        scratch,
        1,
        [scalars, faces, *exchange(faces), *plan, s1, s1, inv],
        10_000_000,
    )
    s3, faces_3 = call(
        functools.partial(step_kernel, 1.0 + C_2 - K_2, K_2 * THETA - C_2, K_2),
        [kept(ROWS), kept(4 * B)],
        scratch,
        1,
        [scalars, faces_2, *exchange(faces_2), *plan, s2, s1, inv],
        10_000_000,
    )
    (residual,) = call(
        residual_kernel,
        [jax.ShapeDtypeStruct((ROWS, LANES), F32)],
        scratch,
        1,
        [scalars, faces_3, *exchange(faces_3), *plan, s3, s1, diag],
        10_000_000,
    )
    return s3.reshape(B, B, LANES), residual.reshape(B, B, LANES)


def solution(mesh):
    leaves, lines = P(None, None, AXES), P(None, AXES)
    return jax.shard_map(
        body,
        mesh=mesh,
        in_specs=(leaves, P(AXES), P(AXES), leaves, lines, lines, lines),
        out_specs=(leaves, leaves),
        check_vma=False,
    )
```

time: 760 us -> 82.7 us (0.11)
  the two profiles are of different devices: /device:TPU:216 before, /device:TPU:40 now
where the time goes in v1:
time: 82.7 us; the launch traced here: 82.3 us
  starting transfers between devices  39.4 us (48%)
  waiting for transfers between devices  25.3 us (31%)
  Pallas kernels  10.5 us (13%)
  local copies, waits for them, and re-layouts  4.96 us (6%)
  between operations  1.46 us (2%)
    ppermute x12, starting transfers between devices, swap(): return lax.ppermute(value, axis, pairs)  22.2 us
    all_to_all x1, starting transfers between devices, body(): lax.all_to_all(jnp.broadcast_to(weight[None], (devices, LANES)), AXES, 0,...  15.2 us
    ppermute x12, waiting for transfers between devices, swap(): return lax.ppermute(value, axis, pairs)  14 us
    all_to_all x1, waiting for transfers between devices, body(): lax.all_to_all(jnp.broadcast_to(weight[None], (devices, LANES)), AXES, 0,...  11.3 us
    pallas_call x4, Pallas kernels, call(): pl.pallas_call(kernel, out_shape=outs, in_specs=specs, out_specs=[pl.Bloc...  10.5 us
    unnamed x11, local copies, waits for them, and re-layouts  4.15 us
    ppermute x1, starting transfers between devices, body(): lax.ppermute(old_coef, AXES, [(i, i + 1) for i in range(devices - 1)])  1.92 us
  transfers between devices with their start and end apart: 14, of which 6 were waited for; matrix products, arithmetic and copies ran while one was open for 3% of the time, Pallas kernels for 0%

profile of v1, /device:TPU:40, one launch (start us, length us, event | category | flops | bytes accessed | tf_op | source)
XLA Modules:
  0.0 82.3 jit_solution(11212573507726191065)
XLA Ops:
  0.6 1.9 %collective-permute-start = (bf16[64,64,128]{2,1,0:T(8,128)(2,1)}, bf16[64,64,128]{2,1,0:T(8,128)(2,1)S(1)}, u32[]{:S(2)}, u32[]{:S(2)}) collective-permute-start(bf16[64,64,128]{2,1,0:T(8,128)(2,1)} %param.7), channel_id=1, source_target_pairs={{0,1},{1,2},{2,3},{3,4},{4,5},{5,6},{6,7},{7,8},{8,9},{9,10},{10,1... | collective-permute-start | bytes 3145736 | tf_op jit(solution)/shard_map/ppermute | solution.py:255
  3.2 0.7 compare_select_fusion
  3.9 0.7 broadcast_in_dim.11
  4.6 15.2 %all-to-all-start = ((s32[256,1,128]{2,1,0:T(1,128)}), s32[256,1,128]{2,1,0:T(1,128)S(1)}, u32[]{:S(2)}, u32[]{:S(2)}) async-start(s32[256,1,128]{2,1,0:T(1,128)} %broadcast_in_dim.11), calls=%async_computation | async-start | bytes 262144 | tf_op jit(solution)/shard_map/all_to_all | solution.py:258
  19.9 0.1 stack.23.position_ref.smem_ref
  20.0 11.3 %all-to-all-done = s32[256,1,128]{2,1,0:T(1,128)S(1)} async-done(((s32[256,1,128]{2,1,0:T(1,128)}), s32[256,1,128]{2,1,0:T(1,128)S(1)}, u32[]{:S(2)}, u32[]{:S(2)}) %all-to-all-start) | async-done | bytes 131104 | tf_op jit(solution)/shard_map/all_to_all | solution.py:258
  31.2 0.0 collective-permute-done
  31.2 0.0 copy-start
  31.2 1.6 %copy-done = f32[64,64,128]{2,1,0:T(8,128)S(1)} copy-done((f32[64,64,128]{2,1,0:T(8,128)S(1)}, f32[64,64,128]{2,1,0:T(8,128)}, u32[]{:S(2)}) %copy-start) | copy-done | bytes 2097176
  32.8 0.0 copy-start.1
  32.8 1.2 %copy-done.1 = bf16[64,64,128]{2,1,0:T(8,128)(2,1)S(1)} copy-done((bf16[64,64,128]{2,1,0:T(8,128)(2,1)S(1)}, bf16[64,64,128]{2,1,0:T(8,128)(2,1)}, u32[]{:S(2)}) %copy-start.1) | copy-done | bytes 1048600
  34.0 0.0 copy-start.2
  34.0 0.0 copy-start.3
  34.1 0.0 copy-start.4
  34.1 2.8 %shard_map.86 = (f32[4096,128]{1,0:T(8,128)S(1)}, f32[4096,128]{1,0:T(8,128)S(1)}, f32[4096,128]{1,0:T(8,128)S(1)}, f32[256,128]{1,0:T(8,128)S(1)}) custom-call(s32[5]{0:T(128)S(1)} %stack.23.position_ref.smem_ref, s32[256,128]{1,0:T(8,128)S(1)} %bitcast.17, bf16[4096,128]{1,0:T(8,128)(2,1)S(1)} %bitcast.16, bf16[4096,128]{1,0:T(8,128)(2,1)S(1)} %bitcast.15, ...), custom_call_target="tpu_custom_call" | custom-call | flops 300000000 | bytes 4194304 | tf_op jit(solution)/shard_map/pallas_call | solution.py:37
  36.8 0.1 collective-permute-start.4
  36.9 1.0 %collective-permute-start.3 = (f32[256,128]{1,0:T(8,128)S(1)}, f32[256,128]{1,0:T(8,128)S(1)}, u32[]{:S(2)}, u32[]{:S(2)}) collective-permute-start(f32[256,128]{1,0:T(8,128)S(1)} %get-tuple-element.10.own_ref), channel_id=1, source_target_pairs={{0,32},{32,0},{64,96},{96,64},{128,160},{160,128},{192,224},{224,1... | collective-permute-start | bytes 393224 | tf_op jit(solution)/shard_map/ppermute | solution.py:243
  38.0 2.3 %collective-permute-start.2 = (f32[256,128]{1,0:T(8,128)S(1)}, f32[256,128]{1,0:T(8,128)S(1)}, u32[]{:S(2)}, u32[]{:S(2)}) collective-permute-start(f32[256,128]{1,0:T(8,128)S(1)} %get-tuple-element.10.own_ref), channel_id=1, source_target_pairs={{32,64},{64,32},{96,128},{128,96},{160,192},{192,160},{33,65},{65,... | collective-permute-start | bytes 393224 | tf_op jit(solution)/shard_map/ppermute | solution.py:243
  40.2 3.7 %collective-permute-start.1 = (f32[256,128]{1,0:T(8,128)S(1)}, f32[256,128]{1,0:T(8,128)S(1)}, u32[]{:S(2)}, u32[]{:S(2)}) collective-permute-start(f32[256,128]{1,0:T(8,128)S(1)} %get-tuple-element.10.own_ref), channel_id=1, source_target_pairs={{1,2},{2,1},{3,4},{4,3},{5,6},{6,5},{7,8},{8,7},{9,10},{10,9},{11,... | collective-permute-start | bytes 393224 | tf_op jit(solution)/shard_map/ppermute | solution.py:243
  44.0 0.0 collective-permute-done.4.refs_3_
  44.0 0.0 collective-permute-done.3.refs_2_
  44.0 1.4 %collective-permute-done.2.refs_1_ = f32[256,128]{1,0:T(8,128)S(1)} collective-permute-done((f32[256,128]{1,0:T(8,128)S(1)}, f32[256,128]{1,0:T(8,128)S(1)}, u32[]{:S(2)}, u32[]{:S(2)}) %collective-permute-start.2) | collective-permute-done | bytes 131104 | tf_op jit(solution)/shard_map/ppermute | solution.py:243
  45.4 3.2 %collective-permute-done.1.refs_0_ = f32[256,128]{1,0:T(8,128)S(1)} collective-permute-done((f32[256,128]{1,0:T(8,128)S(1)}, f32[256,128]{1,0:T(8,128)S(1)}, u32[]{:S(2)}, u32[]{:S(2)}) %collective-permute-start.1) | collective-permute-done | bytes 131104 | tf_op jit(solution)/shard_map/ppermute | solution.py:243
  48.6 0.0 copy-done.2
  48.6 0.0 copy-done.3
  48.6 0.0 copy-done.4
  48.7 2.1 %shard_map.87 = (f32[4096,128]{1,0:T(8,128)S(1)}, f32[256,128]{1,0:T(8,128)S(1)}) custom-call(s32[5]{0:T(128)S(1)} %stack.23.position_ref.smem_ref, f32[256,128]{1,0:T(8,128)S(1)} %get-tuple-element.10.own_ref, f32[256,128]{1,0:T(8,128)S(1)} %collective-permute-done.1.refs_0_, f32[256,128]{1,0:T(8,128)S(1)} %collective-permute-done.2.refs_1_, ...), custom_call_target="tpu_custom_call" | custom-call | flops 10000000 | bytes 4194304 | tf_op jit(solution)/shard_map/pallas_call | solution.py:37
  50.7 0.1 collective-permute-start.8
  50.8 0.1 collective-permute-start.7
  50.9 3.6 %collective-permute-start.6 = (f32[256,128]{1,0:T(8,128)S(1)}, f32[256,128]{1,0:T(8,128)S(1)}, u32[]{:S(2)}, u32[]{:S(2)}) collective-permute-start(f32[256,128]{1,0:T(8,128)S(1)} %get-tuple-element.13.own_ref), channel_id=1, source_target_pairs={{32,64},{64,32},{96,128},{128,96},{160,192},{192,160},{33,65},{65,... | collective-permute-start | bytes 393224 | tf_op jit(solution)/shard_map/ppermute | solution.py:243
  54.5 3.5 %collective-permute-start.5 = (f32[256,128]{1,0:T(8,128)S(1)}, f32[256,128]{1,0:T(8,128)S(1)}, u32[]{:S(2)}, u32[]{:S(2)}) collective-permute-start(f32[256,128]{1,0:T(8,128)S(1)} %get-tuple-element.13.own_ref), channel_id=1, source_target_pairs={{1,2},{2,1},{3,4},{4,3},{5,6},{6,5},{7,8},{8,7},{9,10},{10,9},{11,... | collective-permute-start | bytes 393224 | tf_op jit(solution)/shard_map/ppermute | solution.py:243
  58.0 0.0 collective-permute-done.8.refs_3_
  58.1 0.0 collective-permute-done.7.refs_2_
  58.1 0.6 collective-permute-done.6.refs_1_
  58.6 4.3 %collective-permute-done.5.refs_0_ = f32[256,128]{1,0:T(8,128)S(1)} collective-permute-done((f32[256,128]{1,0:T(8,128)S(1)}, f32[256,128]{1,0:T(8,128)S(1)}, u32[]{:S(2)}, u32[]{:S(2)}) %collective-permute-start.5) | collective-permute-done | bytes 131104 | tf_op jit(solution)/shard_map/ppermute | solution.py:243
  62.9 2.2 %shard_map.88 = (f32[4096,128]{1,0:T(8,128)S(1)}, f32[256,128]{1,0:T(8,128)S(1)}) custom-call(s32[5]{0:T(128)S(1)} %stack.23.position_ref.smem_ref, f32[256,128]{1,0:T(8,128)S(1)} %get-tuple-element.13.own_ref, f32[256,128]{1,0:T(8,128)S(1)} %collective-permute-done.5.refs_0_, f32[256,128]{1,0:T(8,128)S(1)} %collective-permute-done.6.refs_1_, ...), custom_call_target="tpu_custom_call" | custom-call | flops 10000000 | bytes 4194304 | tf_op jit(solution)/shard_map/pallas_call | solution.py:37
  65.1 0.1 collective-permute-start.12
  65.2 0.1 collective-permute-start.11
  65.3 5.1 %collective-permute-start.10 = (f32[256,128]{1,0:T(8,128)S(1)}, f32[256,128]{1,0:T(8,128)S(1)}, u32[]{:S(2)}, u32[]{:S(2)}) collective-permute-start(f32[256,128]{1,0:T(8,128)S(1)} %get-tuple-element.16.own_ref), channel_id=1, source_target_pairs={{32,64},{64,32},{96,128},{128,96},{160,192},{192,160},{33,65},{65,... | collective-permute-start | bytes 393224 | tf_op jit(solution)/shard_map/ppermute | solution.py:243
  70.4 2.5 %collective-permute-start.9 = (f32[256,128]{1,0:T(8,128)S(1)}, f32[256,128]{1,0:T(8,128)S(1)}, u32[]{:S(2)}, u32[]{:S(2)}) collective-permute-start(f32[256,128]{1,0:T(8,128)S(1)} %get-tuple-element.16.own_ref), channel_id=1, source_target_pairs={{1,2},{2,1},{3,4},{4,3},{5,6},{6,5},{7,8},{8,7},{9,10},{10,9},{11,... | collective-permute-start | bytes 393224 | tf_op jit(solution)/shard_map/ppermute | solution.py:243
  73.0 1.3 %copy.9 = f32[64,64,128]{2,1,0:T(8,128)} copy(f32[64,64,128]{2,1,0:T(8,128)S(1)} %bitcast.13) | data formatting | bytes 4194304
  74.3 0.0 collective-permute-done.12.refs_3_
  74.3 0.0 collective-permute-done.11.refs_2_
  74.3 0.0 collective-permute-done.10.refs_1_
  74.3 4.5 %collective-permute-done.9.refs_0_ = f32[256,128]{1,0:T(8,128)S(1)} collective-permute-done((f32[256,128]{1,0:T(8,128)S(1)}, f32[256,128]{1,0:T(8,128)S(1)}, u32[]{:S(2)}, u32[]{:S(2)}) %collective-permute-start.9) | collective-permute-done | bytes 131104 | tf_op jit(solution)/shard_map/ppermute | solution.py:243
  78.8 3.5 %shard_map.89 = f32[4096,128]{1,0:T(8,128)} custom-call(s32[5]{0:T(128)S(1)} %stack.23.position_ref.smem_ref, f32[256,128]{1,0:T(8,128)S(1)} %get-tuple-element.16.own_ref, f32[256,128]{1,0:T(8,128)S(1)} %collective-permute-done.9.refs_0_, f32[256,128]{1,0:T(8,128)S(1)} %collective-permute-done.10.refs_1_, f32[256,128]{1,0:T(8,128)S(1)} %collective-permute-done.11.refs_2_, ...), custom_call_target="tpu_custom_call" | custom-call | flops 10000000 | bytes 4194304 | tf_op jit(solution)/shard_map/pallas_call | solution.py:37
Async XLA Ops:
  0.6 30.6 %collective-permute-start = (bf16[64,64,128]{2,1,0:T(8,128)(2,1)}, bf16[64,64,128]{2,1,0:T(8,128)(2,1)S(1)}, u32[]{:S(2)}, u32[]{:S(2)}) collective-permute-start(bf16[64,64,128]{2,1,0:T(8,128)(2,1)} %param.7), channel_id=1, source_target_pairs={{0,1},{1,2},{2,3},{3,4},{4,5},{5,6},{6,7},{7,8},{8,9},{9,10},{10,1... | collective-permute-start | bytes 3145736 | tf_op jit(solution)/shard_map/ppermute | solution.py:255
  4.6 26.6 %all-to-all-start = ((s32[256,1,128]{2,1,0:T(1,128)}), s32[256,1,128]{2,1,0:T(1,128)S(1)}, u32[]{:S(2)}, u32[]{:S(2)}) async-start(s32[256,1,128]{2,1,0:T(1,128)} %broadcast_in_dim.11), calls=%async_computation | async-start | bytes 262144 | tf_op jit(solution)/shard_map/all_to_all | solution.py:258
  31.2 1.6 %copy-start = (f32[64,64,128]{2,1,0:T(8,128)S(1)}, f32[64,64,128]{2,1,0:T(8,128)}, u32[]{:S(2)}) copy-start(f32[64,64,128]{2,1,0:T(8,128)} %param.10) | copy-start | bytes 6291460
  32.8 1.2 %copy-start.1 = (bf16[64,64,128]{2,1,0:T(8,128)(2,1)S(1)}, bf16[64,64,128]{2,1,0:T(8,128)(2,1)}, u32[]{:S(2)}) copy-start(bf16[64,64,128]{2,1,0:T(8,128)(2,1)} %param.7) | copy-start | bytes 3145732
  34.0 14.6 %copy-start.2 = (s32[4,128]{1,0:T(4,128)S(1)}, s32[4,128]{1,0:T(4,128)}, u32[]{:S(2)}) copy-start(s32[4,128]{1,0:T(4,128)} %refs_4_.5) | copy-start | bytes 6148
  34.0 14.6 %copy-start.3 = (s32[4,128]{1,0:T(4,128)S(1)}, s32[4,128]{1,0:T(4,128)}, u32[]{:S(2)}) copy-start(s32[4,128]{1,0:T(4,128)} %refs_5_.5) | copy-start | bytes 6148
  34.1 14.6 %copy-start.4 = (s32[4,128]{1,0:T(4,128)S(1)}, s32[4,128]{1,0:T(4,128)}, u32[]{:S(2)}) copy-start(s32[4,128]{1,0:T(4,128)} %refs_6_.5) | copy-start | bytes 6148
  36.8 7.2 %collective-permute-start.4 = (f32[256,128]{1,0:T(8,128)S(1)}, f32[256,128]{1,0:T(8,128)S(1)}, u32[]{:S(2)}, u32[]{:S(2)}) collective-permute-start(f32[256,128]{1,0:T(8,128)S(1)} %get-tuple-element.10.own_ref), channel_id=1, source_target_pairs={{0,1},{1,0},{2,3},{3,2},{4,5},{5,4},{6,7},{7,6},{8,9},{9,8},{10,11... | collective-permute-start | bytes 393224 | tf_op jit(solution)/shard_map/ppermute | solution.py:243
  36.9 7.0 %collective-permute-start.3 = (f32[256,128]{1,0:T(8,128)S(1)}, f32[256,128]{1,0:T(8,128)S(1)}, u32[]{:S(2)}, u32[]{:S(2)}) collective-permute-start(f32[256,128]{1,0:T(8,128)S(1)} %get-tuple-element.10.own_ref), channel_id=1, source_target_pairs={{0,32},{32,0},{64,96},{96,64},{128,160},{160,128},{192,224},{224,1... | collective-permute-start | bytes 393224 | tf_op jit(solution)/shard_map/ppermute | solution.py:243
  38.0 7.4 %collective-permute-start.2 = (f32[256,128]{1,0:T(8,128)S(1)}, f32[256,128]{1,0:T(8,128)S(1)}, u32[]{:S(2)}, u32[]{:S(2)}) collective-permute-start(f32[256,128]{1,0:T(8,128)S(1)} %get-tuple-element.10.own_ref), channel_id=1, source_target_pairs={{32,64},{64,32},{96,128},{128,96},{160,192},{192,160},{33,65},{65,... | collective-permute-start | bytes 393224 | tf_op jit(solution)/shard_map/ppermute | solution.py:243
  40.2 8.4 %collective-permute-start.1 = (f32[256,128]{1,0:T(8,128)S(1)}, f32[256,128]{1,0:T(8,128)S(1)}, u32[]{:S(2)}, u32[]{:S(2)}) collective-permute-start(f32[256,128]{1,0:T(8,128)S(1)} %get-tuple-element.10.own_ref), channel_id=1, source_target_pairs={{1,2},{2,1},{3,4},{4,3},{5,6},{6,5},{7,8},{8,7},{9,10},{10,9},{11,... | collective-permute-start | bytes 393224 | tf_op jit(solution)/shard_map/ppermute | solution.py:243
  50.7 7.3 %collective-permute-start.8 = (f32[256,128]{1,0:T(8,128)S(1)}, f32[256,128]{1,0:T(8,128)S(1)}, u32[]{:S(2)}, u32[]{:S(2)}) collective-permute-start(f32[256,128]{1,0:T(8,128)S(1)} %get-tuple-element.13.own_ref), channel_id=1, source_target_pairs={{0,1},{1,0},{2,3},{3,2},{4,5},{5,4},{6,7},{7,6},{8,9},{9,8},{10,11... | collective-permute-start | bytes 393224 | tf_op jit(solution)/shard_map/ppermute | solution.py:243
  50.8 7.2 %collective-permute-start.7 = (f32[256,128]{1,0:T(8,128)S(1)}, f32[256,128]{1,0:T(8,128)S(1)}, u32[]{:S(2)}, u32[]{:S(2)}) collective-permute-start(f32[256,128]{1,0:T(8,128)S(1)} %get-tuple-element.13.own_ref), channel_id=1, source_target_pairs={{0,32},{32,0},{64,96},{96,64},{128,160},{160,128},{192,224},{224,1... | collective-permute-start | bytes 393224 | tf_op jit(solution)/shard_map/ppermute | solution.py:243
  50.9 7.7 %collective-permute-start.6 = (f32[256,128]{1,0:T(8,128)S(1)}, f32[256,128]{1,0:T(8,128)S(1)}, u32[]{:S(2)}, u32[]{:S(2)}) collective-permute-start(f32[256,128]{1,0:T(8,128)S(1)} %get-tuple-element.13.own_ref), channel_id=1, source_target_pairs={{32,64},{64,32},{96,128},{128,96},{160,192},{192,160},{33,65},{65,... | collective-permute-start | bytes 393224 | tf_op jit(solution)/shard_map/ppermute | solution.py:243
  54.5 8.4 %collective-permute-start.5 = (f32[256,128]{1,0:T(8,128)S(1)}, f32[256,128]{1,0:T(8,128)S(1)}, u32[]{:S(2)}, u32[]{:S(2)}) collective-permute-start(f32[256,128]{1,0:T(8,128)S(1)} %get-tuple-element.13.own_ref), channel_id=1, source_target_pairs={{1,2},{2,1},{3,4},{4,3},{5,6},{6,5},{7,8},{8,7},{9,10},{10,9},{11,... | collective-permute-start | bytes 393224 | tf_op jit(solution)/shard_map/ppermute | solution.py:243
  65.1 9.2 %collective-permute-start.12 = (f32[256,128]{1,0:T(8,128)S(1)}, f32[256,128]{1,0:T(8,128)S(1)}, u32[]{:S(2)}, u32[]{:S(2)}) collective-permute-start(f32[256,128]{1,0:T(8,128)S(1)} %get-tuple-element.16.own_ref), channel_id=1, source_target_pairs={{0,1},{1,0},{2,3},{3,2},{4,5},{5,4},{6,7},{7,6},{8,9},{9,8},{10,11... | collective-permute-start | bytes 393224 | tf_op jit(solution)/shard_map/ppermute | solution.py:243
  65.2 9.1 %collective-permute-start.11 = (f32[256,128]{1,0:T(8,128)S(1)}, f32[256,128]{1,0:T(8,128)S(1)}, u32[]{:S(2)}, u32[]{:S(2)}) collective-permute-start(f32[256,128]{1,0:T(8,128)S(1)} %get-tuple-element.16.own_ref), channel_id=1, source_target_pairs={{0,32},{32,0},{64,96},{96,64},{128,160},{160,128},{192,224},{224,1... | collective-permute-start | bytes 393224 | tf_op jit(solution)/shard_map/ppermute | solution.py:243
  65.3 9.0 %collective-permute-start.10 = (f32[256,128]{1,0:T(8,128)S(1)}, f32[256,128]{1,0:T(8,128)S(1)}, u32[]{:S(2)}, u32[]{:S(2)}) collective-permute-start(f32[256,128]{1,0:T(8,128)S(1)} %get-tuple-element.16.own_ref), channel_id=1, source_target_pairs={{32,64},{64,32},{96,128},{128,96},{160,192},{192,160},{33,65},{65,... | collective-permute-start | bytes 393224 | tf_op jit(solution)/shard_map/ppermute | solution.py:243
  70.4 8.4 %collective-permute-start.9 = (f32[256,128]{1,0:T(8,128)S(1)}, f32[256,128]{1,0:T(8,128)S(1)}, u32[]{:S(2)}, u32[]{:S(2)}) collective-permute-start(f32[256,128]{1,0:T(8,128)S(1)} %get-tuple-element.16.own_ref), channel_id=1, source_target_pairs={{1,2},{2,1},{3,4},{4,3},{5,6},{6,5},{7,8},{8,7},{9,10},{10,9},{11,... | collective-permute-start | bytes 393224 | tf_op jit(solution)/shard_map/ppermute | solution.py:243

commit v2 on v1

v2 whole, which is shorter than its diff:
```python
import functools

import jax
import jax.numpy as jnp
from jax import lax
from jax.experimental import pallas as pl
from jax.experimental.pallas import tpu as pltpu
from jax.sharding import PartitionSpec as P

LOWER_BOUND = 0.3
UPPER_BOUND = 1.9
B = 64
ROWS = B * B
LANES = 128
AXES = ("grp", "sfc")

THETA = (UPPER_BOUND + LOWER_BOUND) / 2.0
DELTA = (UPPER_BOUND - LOWER_BOUND) / 2.0
SIGMA = THETA / DELTA
RHO_0 = 1.0 / SIGMA
RHO_1 = 1.0 / (2.0 * SIGMA - RHO_0)
RHO_2 = 1.0 / (2.0 * SIGMA - RHO_1)
C_1, K_1 = RHO_1 * RHO_0, 2.0 * RHO_1 / DELTA
C_2, K_2 = RHO_2 * RHO_1, 2.0 * RHO_2 / DELTA

F32 = jnp.float32
VMEM_LIMIT = 32 * 1024 * 1024


def placed(array, space):
    return array if space in (SMEM, ANY, FREE) else pltpu.with_memory_space_constraint(array, SPACES[space])


def vmem(rows, dtype=F32):
    return pltpu.VMEM((rows, LANES), dtype)


def kept(rows, dtype=F32, lanes=LANES):
    return pltpu.VMEM((rows, lanes), dtype)


def in_hbm(shape):
    return pltpu.HBM(shape, F32)


SMEM, VMEM, HBM, ANY, FREE = "smem", "vmem", "hbm", "any", "free"
SPACES = {FREE: pltpu.VMEM, SMEM: pltpu.SMEM, VMEM: pltpu.VMEM, HBM: pltpu.HBM, ANY: pl.ANY}


def call(kernel, operands, outs, scratch=(), aliases=None, flops=1_000_000):
    specs = [pl.BlockSpec(memory_space=SPACES[space]) for _, space in operands]
    return pl.pallas_call(
        kernel,
        out_shape=[shape for shape, _ in outs],
        in_specs=specs,
        out_specs=[pl.BlockSpec(memory_space=SPACES[space]) for _, space in outs],
        scratch_shapes=list(scratch),
        input_output_aliases=aliases or {},
        compiler_params=pltpu.CompilerParams(vmem_limit_bytes=VMEM_LIMIT),
        cost_estimate=pl.CostEstimate(flops=flops, bytes_accessed=flops, transcendentals=0),
    )(*[placed(array, space) for array, space in operands])


FACE_SLICES = (pl.ds(0, B), pl.ds(ROWS - B, B), pl.ds(0, B, stride=B), pl.ds(B - 1, B, stride=B))
LINES = (0, B // 2 - 1, B // 2, B - 1)


def face(index):
    return pl.ds(index * B, B)


def weights_kernel(count_ref, flags_ref, out_ref):
    slot = lax.broadcasted_iota(jnp.int32, (1, LANES), 1)
    weight = jnp.where(slot < count_ref[0], 1 + 3 * flags_ref[...], 0)
    out_ref[...] = jnp.broadcast_to(weight, out_ref.shape)


def stage_kernel(prev_in, own_in, right_in, staged_ref, prev_ref, own_ref, wide_ref, edge_ref, faces_ref, sems):
    blocks = [
        pltpu.make_async_copy(of, to, sems.at[k])
        for k, (of, to) in enumerate(((prev_in, prev_ref), (own_in, own_ref)))
    ]
    reads = []
    for k in range(2):
        reads.append(pltpu.make_async_copy(right_in.at[k * (B - 1)], faces_ref.at[face(k)], sems.at[2 + k]))
        of = right_in.at[:, pl.ds(k * (B - 8), 8)]
        reads.append(pltpu.make_async_copy(of, edge_ref.at[k], sems.at[4 + k]))
    for read in (*blocks, *reads):
        read.start()
    for side, ref in enumerate((prev_ref, own_ref)):
        blocks[side].wait()
        lanes = slice(side * LANES, (side + 1) * LANES)
        wide_ref[...] = ref[...].astype(F32)
        for k, line in enumerate(LINES):
            staged_ref[face(k), lanes] = ref[face(line)]
            staged_ref[face(4 + k), lanes] = wide_ref[pl.ds(line, B, stride=B)].astype(jnp.bfloat16)
    for read in reads:
        read.wait()
    for k in range(2):
        faces_ref[face(2 + k)] = edge_ref[k, :, 7 * k, :]
    left = jnp.concatenate([faces_ref[0 : 2 * B], faces_ref[2 * B : 4 * B]], axis=1)
    for piece in range(3):
        part = left.astype(jnp.bfloat16)
        staged_ref[(8 + 2 * piece) * B : (10 + 2 * piece) * B] = part
        left = left - part.astype(F32)


def lane_plan(position, weights_ref):
    rows = lax.broadcasted_iota(jnp.int32, weights_ref.shape, 0)
    before = jnp.where(rows < position, weights_ref[...], 0).astype(F32)
    made = jnp.sum(jnp.sum(before, axis=0, keepdims=True), axis=1, keepdims=True)
    drift = made - (position * LANES).astype(F32)
    own = weights_ref[pl.ds(position, 1), :].astype(F32)
    prev = weights_ref[pl.ds(jnp.maximum(position - 1, 0), 1), :].astype(F32)
    prev = jnp.where(position > 0, prev, 0.0)
    window = 2 * LANES
    spread = jnp.broadcast_to(jnp.concatenate([prev, own], axis=1), (LANES, window)).astype(jnp.bfloat16)
    slot = lax.broadcasted_iota(jnp.int32, (window, window), 0)
    other = lax.broadcasted_iota(jnp.int32, (window, window), 1)
    lower = jnp.where(other <= slot, 1.0, 0.0).astype(jnp.bfloat16)
    inclusive = lax.dot_general(
        lower, spread, (((1,), (1,)), ((), ())), preferred_element_type=F32
    )
    before_own = inclusive[LANES - 1 : LANES]
    inclusive = inclusive - before_own
    target = lax.broadcasted_iota(jnp.int32, (1, LANES), 1).astype(F32) - drift
    passed = inclusive <= target
    parent = jnp.sum(jnp.where(passed, 1.0, 0.0), axis=0, keepdims=True)
    start = jnp.max(jnp.where(passed, inclusive, -before_own), axis=0, keepdims=True)
    stop = jnp.min(jnp.where(passed, 1e6, inclusive), axis=0, keepdims=True)
    child = target - start
    slot_f = lax.broadcasted_iota(jnp.int32, (window, LANES), 0).astype(F32)
    one_hot = jnp.where(slot_f == parent, 1.0, 0.0).astype(jnp.bfloat16)
    refined = jnp.where((stop - start) > 2.0, 1.0, 0.0)
    first_bit = jnp.where((child == 1.0) | (child == 3.0), 1.0, 0.0)
    second_bit = jnp.where(child >= 2.0, 1.0, 0.0)
    return one_hot, refined, first_bit, second_bit


def face_kernel(scalar_ref, weights_ref, staged_ref, faces_ref, one_hot_ref, flags_ref, dup_ref):
    one_hot, refined, first_bit, second_bit = lane_plan(scalar_ref[0], weights_ref)
    one_hot_ref[...] = one_hot
    flags_ref[...] = jnp.concatenate(
        [refined, first_bit, second_bit, jnp.zeros((5, LANES), F32)], axis=0
    )
    lines = staged_ref[0 : 8 * B]
    picked = jnp.dot(lines, one_hot, preferred_element_type=F32)
    half = B // 2
    bits = (first_bit > 0.0, second_bit > 0.0)
    for k in range(4):
        base = 4 * B * (k // 2)
        along, side = bits[1 - k // 2], bits[k // 2]
        line = [picked[base + i * B : base + (i + 1) * B] for i in range(4)]
        low, high, plain = ((line[0], line[2], line[0]), (line[1], line[3], line[3]))[k % 2]
        chosen = jnp.where(side, high, low)
        chosen = jnp.where(along, chosen[half:], chosen[:half])
        dup_ref[pl.ds(k * B, half, stride=2)] = chosen
        dup_ref[pl.ds(k * B + 1, half, stride=2)] = chosen
        coefficient = jnp.where(refined > 0.0, dup_ref[face(k)], plain)
        lanes = slice((k // 2) * LANES, (k // 2 + 1) * LANES)
        high, middle, low = (staged_ref[face(8 + 2 * i + k % 2), lanes].astype(F32) for i in range(3))
        right = high + (middle + low)
        faces_ref[face(k)] = right / (4.0 + coefficient) * (1.0 / THETA)


def sweep(field_ref, finish):
    edge = lax.broadcasted_iota(jnp.int32, (B, LANES), 0)
    is_first, is_last = edge == 0, edge == B - 1

    def plane(index, position):
        start = pl.multiple_of(index * B, B)
        at = pl.ds(start, B)
        centre = field_ref[at]
        if position == 0:
            total = field_ref[pl.ds((index + 1) * B, B)]
            left = pltpu.roll(centre, 1, 0)
        else:
            total = field_ref[pl.ds(pl.multiple_of((index - 1) * B, B), B)]
            left = field_ref[pl.ds(index * B - 1, B)]
        if position == 1:
            total = total + field_ref[pl.ds(pl.multiple_of((index + 1) * B, B), B)]
        if position == 2:
            right = pltpu.roll(centre, B - 1, 0)
        else:
            right = field_ref[pl.ds(index * B + 1, B)]
        total = total + jnp.where(is_first, 0.0, left) + jnp.where(is_last, 0.0, right)
        finish(at, centre, total)

    plane(0, 0)

    def step(index, carry):
        plane(index, 1)
        return carry

    lax.fori_loop(1, B - 1, step, 0, unroll=2)
    plane(B - 1, 2)


def build_kernel(prev_ref, own_ref, right_in, one_hot_ref, flags_ref, s_ref, inv_ref, diag_ref, part_ref, part_faces_ref, inv_faces_ref, right_ref, pick_ref, dup_ref, sem):
    read = pltpu.make_async_copy(right_in, right_ref, sem)
    read.start()
    chunk = ROWS // 8
    one_hot = one_hot_ref[...]
    refined, first_bit, second_bit = (flags_ref[i : i + 1] > 0.0 for i in range(3))

    def pick(step, carry):
        at = pl.ds(pl.multiple_of(step * chunk, chunk), chunk)
        both = jnp.concatenate([prev_ref[at], own_ref[at]], axis=1)
        pick_ref[at] = jnp.dot(both, one_hot, preferred_element_type=F32)
        return carry

    lax.fori_loop(0, ROWS // chunk, pick, 0, unroll=2)
    read.wait()
    half = B // 2

    def leaf(row, carry):
        low = pick_ref[pl.ds(pl.multiple_of(row * B, B), B)]
        high = pick_ref[pl.ds(pl.multiple_of((row + half) * B, B), B)]
        chosen = jnp.where(first_bit, high, low)
        chosen = jnp.where(second_bit, chosen[half:], chosen[:half])
        slot = pl.multiple_of((row % 2) * B, B)
        dup_ref[pl.ds(slot, half, stride=2)] = chosen
        dup_ref[pl.ds(slot + 1, half, stride=2)] = chosen
        doubled = dup_ref[pl.ds(slot, B)]
        for k in range(2):
            at = pl.ds(pl.multiple_of((2 * row + k) * B, B), B)
            diag = 4.0 + jnp.where(refined, doubled, pick_ref[at])
            inv = 1.0 / diag
            diag_ref[at] = diag
            inv_ref[at] = inv
            s_ref[at] = right_ref[at] * inv * (1.0 / THETA)
        return carry

    lax.fori_loop(0, half, leaf, 0, unroll=2)

    def finish(at, centre, total):
        part_ref[at] = (1.0 + C_1 + K_1 * (THETA - 1.0)) * centre + K_1 * (inv_ref[at] * total)

    sweep(s_ref, finish)
    for k, at in enumerate(FACE_SLICES):
        part_faces_ref[face(k)] = part_ref[at]
        inv_faces_ref[face(k)] = inv_ref[at]


def fill_ghosts(scalar_ref, source_refs, first_ref, second_ref, kind_ref, ghost_ref, pair_ref):
    position = scalar_ref[0]
    half = B // 2
    for side in range(4):
        kind = kind_ref[side : side + 1]
        values = []
        for index_ref in (first_ref, second_ref):
            index = index_ref[side : side + 1]
            offset = lax.shift_right_logical(index, 7) - position
            lane = jnp.broadcast_to(index & (LANES - 1), (B, LANES))
            value = jnp.zeros((B, LANES), F32)
            for i, source_ref in enumerate(source_refs):
                taken = jnp.take_along_axis(
                    source_ref[face(side ^ 1)], lane, axis=1, mode="promise_in_bounds"
                )
                value = jnp.where(offset == scalar_ref[1 + i], taken, value)
            values.append(value)
        leading, second = values
        at = side * 4 * B
        pair_ref[at : at + B] = leading
        pair_ref[at + B : at + 2 * B] = second
        mean_low = (pair_ref[pl.ds(at, half, stride=2)] + pair_ref[pl.ds(at + 1, half, stride=2)]) * 0.5
        mean_high = (
            pair_ref[pl.ds(at + B, half, stride=2)] + pair_ref[pl.ds(at + B + 1, half, stride=2)]
        ) * 0.5
        for part in range(2):
            for odd in range(2):
                pair_ref[pl.ds(at + (2 + part) * B + odd, half, stride=2)] = leading[
                    part * half : (part + 1) * half
                ]
        ghost = jnp.where(kind == 4, jnp.concatenate([mean_low, mean_high], axis=0), 0.0)
        ghost = jnp.where(kind == 1, leading, ghost)
        ghost = jnp.where(kind == 2, pair_ref[at + 2 * B : at + 3 * B], ghost)
        ghost = jnp.where(kind == 3, pair_ref[at + 3 * B : at + 4 * B], ghost)
        ghost_ref[face(side)] = ghost


CORNERS = (
    ((0, 0), (2, 0)),
    ((0, B - 1), (3, 0)),
    ((1, 0), (2, B - 1)),
    ((1, B - 1), (3, B - 1)),
)


def step_faces_kernel(scale, scalar_ref, own_ref, *refs):
    sources, (first_ref, second_ref, kind_ref, part_ref, inv_ref, out_ref, ghost_ref, sum_ref, pair_ref) = (
        (own_ref, *refs[:4]),
        refs[4:],
    )
    fill_ghosts(scalar_ref, sources, first_ref, second_ref, kind_ref, ghost_ref, pair_ref)
    sum_ref[...] = ghost_ref[...]
    for one, two in CORNERS:
        for (at_face, at_row), (of_face, of_row) in ((one, two), (two, one)):
            at, of = at_face * B + at_row, of_face * B + of_row
            sum_ref[at : at + 1] = sum_ref[at : at + 1] + ghost_ref[of : of + 1]
    out_ref[...] = part_ref[...] + scale * (inv_ref[...] * sum_ref[...])


def step_block_kernel(faces_ref, old_ref, u_ref, inv_ref, v_ref, part_ref, part_faces_ref):
    for k, at in enumerate(FACE_SLICES):
        v_ref[at] = faces_ref[face(k)]

    def finish(at, centre, total):
        part_ref[at] = (
            (1.0 + C_2 - K_2) * centre + (K_2 * THETA - C_2) * u_ref[at] + K_2 * (inv_ref[at] * total)
        )

    sweep(v_ref, finish)
    for k, at in enumerate(FACE_SLICES):
        part_faces_ref[face(k)] = part_ref[at]


def last_block_kernel(faces_ref, old_ref, right_ref, diag_ref, v_ref, out_ref, residual_ref, edge_ref, part_ref, sems):
    for k, at in enumerate(FACE_SLICES):
        v_ref[at] = faces_ref[face(k)]
    write = pltpu.make_async_copy(v_ref, out_ref, sems.at[0])
    write.start()

    def finish(at, centre, total):
        part_ref[at] = right_ref[at] - diag_ref[at] * centre + total

    sweep(v_ref, finish)
    write_residual = pltpu.make_async_copy(part_ref, residual_ref, sems.at[1])
    write_residual.start()
    edge_ref[0:B] = part_ref[0:B]
    edge_ref[B : 2 * B] = part_ref[ROWS - B : ROWS]
    for plane in range(B):
        for k, tile in enumerate((0, B - 8)):
            to = 2 * B + k * 8 * B + plane * 8
            edge_ref[to : to + 8] = part_ref[plane * B + tile : plane * B + tile + 8]
    write.wait()
    write_residual.wait()


def last_faces_kernel(scalar_ref, own_ref, *refs):
    sources, refs = (own_ref, *refs[:4]), refs[4:]
    first_ref, second_ref, kind_ref, edge_ref, _, out_ref, ghost_ref, pair_ref, sum_ref, sems = refs
    fill_ghosts(scalar_ref, sources, first_ref, second_ref, kind_ref, ghost_ref, pair_ref)
    sum_ref[...] = edge_ref[...]
    sum_ref[0 : 2 * B] = sum_ref[0 : 2 * B] + ghost_ref[0 : 2 * B]
    for (at_face, at_row), (of_face, of_row) in CORNERS:
        at, of = at_face * B + at_row, of_face * B + of_row
        sum_ref[at : at + 1] = sum_ref[at : at + 1] + ghost_ref[of : of + 1]
    copies = []
    for k in range(2):
        tiles = 2 * B + k * 8 * B
        at = pl.ds(tiles + 7 * k, B, stride=8)
        sum_ref[at] = sum_ref[at] + ghost_ref[face(2 + k)]
        copies.append((face(k), pl.ds(k * (ROWS - B), B)))
    copies = [
        pltpu.make_async_copy(sum_ref.at[of], out_ref.at[to], sems.at[k]) for k, (of, to) in enumerate(copies)
    ]
    cells = out_ref.reshape(B, B, LANES)
    for k in range(2):
        tiles = sum_ref.at[pl.ds(2 * B + k * 8 * B + 8, 8 * (B - 2))].reshape(B - 2, 8, LANES)
        copies.append(
            pltpu.make_async_copy(tiles, cells.at[pl.ds(1, B - 2), pl.ds(k * (B - 8), 8)], sems.at[2 + k])
        )
    for copy in copies:
        copy.start()
    for copy in copies:
        copy.wait()


def swap(value, axis, parity):
    count = lax.axis_size(axis)
    pairs = []
    for low in range(parity, count - 1, 2):
        pairs += [(low, low + 1), (low + 1, low)]
    return lax.ppermute(value, axis, pairs)


def exchange(faces):
    received = [swap(faces, "sfc", 0), swap(faces, "grp", 0), swap(faces, "grp", 1), swap(faces, "sfc", 1)]
    return [(array, VMEM) for array in (faces, *received)]


def body(old_coef, refine_flags, counts, right_side, nbr_first, nbr_second, face_kind):
    grp, sfc = lax.axis_index("grp"), lax.axis_index("sfc")
    n_sfc = lax.axis_size("sfc")
    devices = lax.axis_size(AXES)
    position = grp * n_sfc + sfc
    right = right_side.reshape(ROWS, LANES)
    flags = refine_flags.reshape(1, LANES)
    own = old_coef.reshape(ROWS, LANES)
    prev = lax.ppermute(own, AXES, [(i, i + 1) for i in range(devices - 1)])
    (spread,) = call(
        weights_kernel,
        [(counts, SMEM), (flags, VMEM)],
        [(kept(devices, jnp.int32), VMEM)],
    )
    weights = lax.all_to_all(spread, AXES, 0, 0, tiled=True)
    even_sfc, even_grp = 1 - 2 * (sfc % 2), n_sfc * (1 - 2 * (grp % 2))
    scalars = jnp.stack([position, 0, even_sfc, even_grp, -even_grp, -even_sfc]).astype(jnp.int32)

    staged, prev, own = call(
        stage_kernel,
        [(prev, ANY), (own, HBM), (right_side, HBM)],
        [(kept(14 * B, jnp.bfloat16, 2 * LANES), VMEM)] + [(kept(ROWS, jnp.bfloat16), VMEM)] * 2,
        [vmem(ROWS), pltpu.VMEM((2, B, 8, LANES), F32), vmem(4 * B), pltpu.SemaphoreType.DMA((6,))],
        flops=8_000_000,
    )
    faces, one_hot, flags = call(
        face_kernel,
        [(scalars, SMEM), (weights, FREE), (staged, FREE)],
        [(kept(4 * B), VMEM), (kept(2 * LANES, jnp.bfloat16), VMEM), (kept(8), VMEM)],
        [vmem(4 * B)],
    )
    neighbours = exchange(faces)
    s1, inv, diag, part, part_faces, inv_faces, right = call(
        build_kernel,
        [(prev, VMEM), (own, VMEM), (right, HBM), (one_hot, VMEM), (flags, VMEM)],
        [(kept(ROWS), VMEM)] * 4 + [(kept(4 * B), VMEM)] * 2 + [(kept(ROWS), VMEM)],
        [vmem(ROWS), vmem(2 * B), pltpu.SemaphoreType.DMA],
        flops=8_000_000,
    )
    plan = [(nbr_first, VMEM), (nbr_second, VMEM), (face_kind, VMEM)]
    ghost_scratch = [vmem(4 * B), vmem(4 * B), vmem(16 * B)]
    (faces,) = call(
        functools.partial(step_faces_kernel, K_1),
        [(scalars, SMEM), *neighbours, *plan, (part_faces, VMEM), (inv_faces, VMEM)],
        [(kept(4 * B), VMEM)],
        ghost_scratch,
    )
    neighbours = exchange(faces)
    _, part, part_faces = call(
        step_block_kernel,
        [(faces, VMEM), (part, VMEM), (s1, VMEM), (inv, VMEM)],
        [(kept(ROWS), VMEM), (kept(ROWS), VMEM), (kept(4 * B), VMEM)],
        aliases={1: 0},
        flops=8_000_000,
    )
    (faces,) = call(
        functools.partial(step_faces_kernel, K_2),
        [(scalars, SMEM), *neighbours, *plan, (part_faces, VMEM), (inv_faces, VMEM)],
        [(kept(4 * B), VMEM)],
        ghost_scratch,
    )
    neighbours = exchange(faces)
    _, iterate, residual, edges = call(
        last_block_kernel,
        [(faces, VMEM), (part, VMEM), (right, VMEM), (diag, VMEM)],
        [(kept(ROWS), VMEM), (in_hbm((ROWS, LANES)), HBM), (in_hbm((ROWS, LANES)), HBM), (kept(18 * B), VMEM)],
        [vmem(ROWS), pltpu.SemaphoreType.DMA((2,))],
        aliases={1: 0},
        flops=8_000_000,
    )
    (residual,) = call(
        last_faces_kernel,
        [(scalars, SMEM), *neighbours, *plan, (edges, VMEM), (residual, HBM)],
        [(in_hbm((ROWS, LANES)), HBM)],
        [vmem(4 * B), vmem(16 * B), vmem(18 * B), pltpu.SemaphoreType.DMA((4,))],
        aliases={10: 0},
    )
    return iterate.reshape(B, B, LANES), residual.reshape(B, B, LANES)


def solution(mesh):
    leaves, lines = P(None, None, AXES), P(None, AXES)
    return jax.shard_map(
        body,
        mesh=mesh,
        in_specs=(leaves, P(AXES), P(AXES), leaves, lines, lines, lines),
        out_specs=(leaves, leaves),
        check_vma=False,
    )
```

time: 82.7 us -> 72 us (0.87)
  waiting for transfers between devices: 25.3 us -> 16.6 us
  Pallas kernels: 10.5 us -> 14.1 us
  starting transfers between devices: 39.4 us -> 36.8 us
  local copies, waits for them, and re-layouts: 4.96 us -> 2.53 us
    ppermute x12, waiting for transfers between devices: 14 us -> 7.69 us  [swap(): return lax.ppermute(value, axis, pairs)]
    pallas_call x4 -> x9, Pallas kernels: 10.5 us -> 14.1 us  [call(): pl.pallas_call(kernel, out_shape=[shape for shape, _ in outs], in_specs=s...]
    ppermute x12, starting transfers between devices: 22.2 us -> 19.7 us  [swap(): return lax.ppermute(value, axis, pairs)]
    all_to_all x1, waiting for transfers between devices: 11.3 us -> 8.87 us  [body(): weights = lax.all_to_all(spread, AXES, 0, 0, tiled=True)]
    unnamed x11 -> x12, local copies, waits for them, and re-layouts: 4.15 us -> 2.45 us
  transfers between devices with their start and end apart: 14 -> 14, of which waited for: 6 -> 8; matrix products, arithmetic and copies ran while one was open for 3% -> 0% of each run, Pallas kernels for 0% -> 13%
where the time goes in v2:
time: 72 us; the launch traced here: 71.5 us
  starting transfers between devices  36.8 us (51%)
  waiting for transfers between devices  16.6 us (23%)
  Pallas kernels  14.1 us (20%)
  local copies, waits for them, and re-layouts  2.53 us (4%)
  between operations  1.53 us (2%)
    ppermute x12, starting transfers between devices, swap(): return lax.ppermute(value, axis, pairs)  19.7 us
    all_to_all x1, starting transfers between devices, body(): weights = lax.all_to_all(spread, AXES, 0, 0, tiled=True)  15.2 us
    pallas_call x9, Pallas kernels, call(): pl.pallas_call(kernel, out_shape=[shape for shape, _ in outs], in_specs=s...  14.1 us
    all_to_all x1, waiting for transfers between devices, body(): weights = lax.all_to_all(spread, AXES, 0, 0, tiled=True)  8.87 us
    ppermute x12, waiting for transfers between devices, swap(): return lax.ppermute(value, axis, pairs)  7.69 us
    unnamed x12, local copies, waits for them, and re-layouts  2.45 us
    ppermute x1, starting transfers between devices, body(): prev = lax.ppermute(own, AXES, [(i, i + 1) for i in range(devices - 1)])  1.92 us
  transfers between devices with their start and end apart: 14, of which 8 were waited for; matrix products, arithmetic and copies ran while one was open for 0% of the time, Pallas kernels for 13%

profile of v2, /device:TPU:40, one launch (start us, length us, event | category | flops | bytes accessed | tf_op | source)
XLA Modules:
  0.0 71.5 jit_solution(10269726320133824914)
XLA Ops:
  0.6 1.9 %collective-permute-start = (bf16[4096,128]{1,0:T(8,128)(2,1)}, bf16[4096,128]{1,0:T(8,128)(2,1)S(1)}, u32[]{:S(2)}, u32[]{:S(2)}) collective-permute-start(bf16[4096,128]{1,0:T(8,128)(2,1)} %bitcast.18), channel_id=1, source_target_pairs={{0,1},{1,2},{2,3},{3,4},{4,5},{5,6},{6,7},{7,8},{8,9},{9,10},{10,1... | collective-permute-start | bytes 3145736 | tf_op jit(solution)/shard_map/ppermute | solution.py:391
  3.2 0.0 copy-start.5
  3.2 0.6 copy-done.5
  3.9 0.7 shard_map.86
  4.5 15.2 %all-to-all-start = ((s32[256,1,128]{2,1,0:T(1,128)}), s32[256,1,128]{2,1,0:T(1,128)S(1)}, u32[]{:S(2)}, u32[]{:S(2)}) async-start(s32[256,1,128]{2,1,0:T(1,128)} %bitcast.7), calls=%async_computation | async-start | bytes 262144 | tf_op jit(solution)/shard_map/all_to_all | solution.py:397
  19.8 0.1 stack.23.scalar_ref
  19.9 0.0 collective-permute-done.prev_in
  19.9 1.6 %shard_map.87 = (bf16[896,256]{1,0:T(8,128)(2,1)S(1)}, bf16[4096,128]{1,0:T(8,128)(2,1)S(1)}, bf16[4096,128]{1,0:T(8,128)(2,1)S(1)}) custom-call(bf16[4096,128]{1,0:T(8,128)(2,1)S(1)} %collective-permute-done.prev_in, bf16[4096,128]{1,0:T(8,128)(2,1)} %bitcast.19, f32[64,64,128]{2,1,0:T(8,128)} %right_in.1), custom_call_target="tpu_custom_call" | custom-call | flops 8000000 | bytes 8000000 | tf_op jit(solution)/shard_map/pallas_call | solution.py:52
  21.5 0.0 copy-start
  21.5 0.8 %copy-done = bf16[896,256]{1,0:T(8,128)(2,1)} copy-done((bf16[896,256]{1,0:T(8,128)(2,1)}, bf16[896,256]{1,0:T(8,128)(2,1)S(1)}, u32[]{:S(2)}) %copy-start) | copy-done | bytes 458776
  22.3 8.9 %all-to-all-done = s32[256,1,128]{2,1,0:T(1,128)S(1)} async-done(((s32[256,1,128]{2,1,0:T(1,128)}), s32[256,1,128]{2,1,0:T(1,128)S(1)}, u32[]{:S(2)}, u32[]{:S(2)}) %all-to-all-start) | async-done | bytes 131104 | tf_op jit(solution)/shard_map/all_to_all | solution.py:397
  31.2 0.0 copy-start.1
  31.2 1.0 %copy-done.1 = bf16[896,256]{1,0:T(8,128)(2,1)S(1)} copy-done((bf16[896,256]{1,0:T(8,128)(2,1)S(1)}, bf16[896,256]{1,0:T(8,128)(2,1)}, u32[]{:S(2)}) %copy-start.1) | copy-done | bytes 458776
  32.2 1.0 %shard_map.88 = (f32[256,128]{1,0:T(8,128)S(1)}, bf16[256,128]{1,0:T(8,128)(2,1)S(1)}, f32[8,128]{1,0:T(8,128)S(1)}) custom-call(s32[6]{0:T(128)S(1)} %stack.23.scalar_ref, s32[256,128]{1,0:T(8,128)S(1)} %bitcast.14, bf16[896,256]{1,0:T(8,128)(2,1)S(1)} %copy-done.1), custom_call_target="tpu_custom_call" | custom-call | flops 1000000 | bytes 1000000 | tf_op jit(solution)/shard_map/pallas_call | solution.py:52
  33.2 3.3 %collective-permute-start.4 = (f32[256,128]{1,0:T(8,128)S(1)}, f32[256,128]{1,0:T(8,128)S(1)}, u32[]{:S(2)}, u32[]{:S(2)}) collective-permute-start(f32[256,128]{1,0:T(8,128)S(1)} %get-tuple-element.21.own_ref), channel_id=1, source_target_pairs={{1,2},{2,1},{3,4},{4,3},{5,6},{6,5},{7,8},{8,7},{9,10},{10,9},{11,... | collective-permute-start | bytes 393224 | tf_op jit(solution)/shard_map/ppermute | solution.py:375
  36.6 2.6 %collective-permute-start.3 = (f32[256,128]{1,0:T(8,128)S(1)}, f32[256,128]{1,0:T(8,128)S(1)}, u32[]{:S(2)}, u32[]{:S(2)}) collective-permute-start(f32[256,128]{1,0:T(8,128)S(1)} %get-tuple-element.21.own_ref), channel_id=1, source_target_pairs={{32,64},{64,32},{96,128},{128,96},{160,192},{192,160},{33,65},{65,... | collective-permute-start | bytes 393224 | tf_op jit(solution)/shard_map/ppermute | solution.py:375
  39.2 0.1 collective-permute-start.2
  39.3 0.1 collective-permute-start.1
  39.4 0.0 copy-start.2
  39.4 0.0 copy-start.3
  39.5 0.0 copy-start.4
  39.5 3.4 %shard_map.89 = (f32[4096,128]{1,0:T(8,128)S(1)}, f32[4096,128]{1,0:T(8,128)S(1)}, f32[4096,128]{1,0:T(8,128)S(1)}, f32[4096,128]{1,0:T(8,128)S(1)}, f32[256,128...) custom-call(bf16[4096,128]{1,0:T(8,128)(2,1)S(1)} %get-tuple-element.22.prev_ref, ...), custom_call_target="tpu_custom_call" | custom-call | flops 8000000 | bytes 8000000 | tf_op jit(solution)/shard_map/pallas_call | solution.py:52
  42.9 0.0 collective-permute-done.4.refs_3_
  42.9 0.6 collective-permute-done.3.refs_2_
  43.5 0.8 %collective-permute-done.2.refs_1_ = f32[256,128]{1,0:T(8,128)S(1)} collective-permute-done((f32[256,128]{1,0:T(8,128)S(1)}, f32[256,128]{1,0:T(8,128)S(1)}, u32[]{:S(2)}, u32[]{:S(2)}) %collective-permute-start.2) | collective-permute-done | bytes 131104 | tf_op jit(solution)/shard_map/ppermute | solution.py:375
  44.3 0.0 collective-permute-done.1.refs_0_
  44.3 0.0 copy-done.2
  44.3 0.0 copy-done.3
  44.3 0.0 copy-done.4
  44.3 1.0 %shard_map.90.faces_ref.own_ref = f32[256,128]{1,0:T(8,128)S(1)} custom-call(s32[6]{0:T(128)S(1)} %stack.23.scalar_ref, f32[256,128]{1,0:T(8,128)S(1)} %get-tuple-element.21.own_ref, f32[256,128]{1,0:T(8,128)S(1)} %collective-permute-done.1.refs_0_, f32[256,128]{1,0:T(8,128)S(1)} %collective-permute-done.2.refs_1_, ...), custom_call_target="tpu_custom_call" | custom-call | flops 1000000 | bytes 1000000 | tf_op jit(solution)/shard_map/pallas_call | solution.py:52
  45.3 3.5 %collective-permute-start.8 = (f32[256,128]{1,0:T(8,128)S(1)}, f32[256,128]{1,0:T(8,128)S(1)}, u32[]{:S(2)}, u32[]{:S(2)}) collective-permute-start(f32[256,128]{1,0:T(8,128)S(1)} %shard_map.90.faces_ref.own_ref), channel_id=1, source_target_pairs={{1,2},{2,1},{3,4},{4,3},{5,6},{6,5},{7,8},{8,7},{9,10},{10,9},{11,... | collective-permute-start | bytes 393224 | tf_op jit(solution)/shard_map/ppermute | solution.py:375
  48.9 3.5 %collective-permute-start.7 = (f32[256,128]{1,0:T(8,128)S(1)}, f32[256,128]{1,0:T(8,128)S(1)}, u32[]{:S(2)}, u32[]{:S(2)}) collective-permute-start(f32[256,128]{1,0:T(8,128)S(1)} %shard_map.90.faces_ref.own_ref), channel_id=1, source_target_pairs={{32,64},{64,32},{96,128},{128,96},{160,192},{192,160},{33,65},{65,... | collective-permute-start | bytes 393224 | tf_op jit(solution)/shard_map/ppermute | solution.py:375
  52.4 0.1 collective-permute-start.6
  52.5 0.1 collective-permute-start.5
  52.6 1.1 %shard_map.91 = (f32[4096,128]{1,0:T(8,128)S(1)}, f32[4096,128]{1,0:T(8,128)S(1)}, f32[256,128]{1,0:T(8,128)S(1)}) custom-call(f32[256,128]{1,0:T(8,128)S(1)} %shard_map.90.faces_ref.own_ref, f32[4096,128]{1,0:T(8,128)S(1)} %get-tuple-element.28.old_ref, f32[4096,128]{1,0:T(8,128)S(1)} %get-tuple-element.29.u_ref, ...), custom_call_target="tpu_custom_call", output_to_operand_aliasing={{0}: (1, {})} | custom-call | flops 8000000 | bytes 8000000 | tf_op jit(solution)/shard_map/pallas_call | solution.py:52
  53.6 0.1 collective-permute-done.8.refs_3_
  53.7 2.0 %collective-permute-done.7.refs_2_ = f32[256,128]{1,0:T(8,128)S(1)} collective-permute-done((f32[256,128]{1,0:T(8,128)S(1)}, f32[256,128]{1,0:T(8,128)S(1)}, u32[]{:S(2)}, u32[]{:S(2)}) %collective-permute-start.7) | collective-permute-done | bytes 131104 | tf_op jit(solution)/shard_map/ppermute | solution.py:375
  55.7 1.7 %collective-permute-done.6.refs_1_ = f32[256,128]{1,0:T(8,128)S(1)} collective-permute-done((f32[256,128]{1,0:T(8,128)S(1)}, f32[256,128]{1,0:T(8,128)S(1)}, u32[]{:S(2)}, u32[]{:S(2)}) %collective-permute-start.6) | collective-permute-done | bytes 131104 | tf_op jit(solution)/shard_map/ppermute | solution.py:375
  57.4 0.0 collective-permute-done.5.refs_0_
  57.4 1.0 %shard_map.92.faces_ref.own_ref = f32[256,128]{1,0:T(8,128)S(1)} custom-call(s32[6]{0:T(128)S(1)} %stack.23.scalar_ref, f32[256,128]{1,0:T(8,128)S(1)} %shard_map.90.faces_ref.own_ref, f32[256,128]{1,0:T(8,128)S(1)} %collective-permute-done.5.refs_0_, f32[256,128]{1,0:T(8,128)S(1)} %collective-permute-done.6.refs_1_, ...), custom_call_target="tpu_custom_call" | custom-call | flops 1000000 | bytes 1000000 | tf_op jit(solution)/shard_map/pallas_call | solution.py:52
  58.5 3.7 %collective-permute-start.12 = (f32[256,128]{1,0:T(8,128)S(1)}, f32[256,128]{1,0:T(8,128)S(1)}, u32[]{:S(2)}, u32[]{:S(2)}) collective-permute-start(f32[256,128]{1,0:T(8,128)S(1)} %shard_map.92.faces_ref.own_ref), channel_id=1, source_target_pairs={{1,2},{2,1},{3,4},{4,3},{5,6},{6,5},{7,8},{8,7},{9,10},{10,9},{11,... | collective-permute-start | bytes 393224 | tf_op jit(solution)/shard_map/ppermute | solution.py:375
  62.2 2.4 %collective-permute-start.11 = (f32[256,128]{1,0:T(8,128)S(1)}, f32[256,128]{1,0:T(8,128)S(1)}, u32[]{:S(2)}, u32[]{:S(2)}) collective-permute-start(f32[256,128]{1,0:T(8,128)S(1)} %shard_map.92.faces_ref.own_ref), channel_id=1, source_target_pairs={{32,64},{64,32},{96,128},{128,96},{160,192},{192,160},{33,65},{65,... | collective-permute-start | bytes 393224 | tf_op jit(solution)/shard_map/ppermute | solution.py:375
  64.6 0.1 collective-permute-start.10
  64.7 0.1 collective-permute-start.9
  64.8 2.3 %shard_map.93 = (f32[4096,128]{1,0:T(8,128)S(1)}, f32[4096,128]{1,0:T(8,128)}, f32[4096,128]{1,0:T(8,128)}, f32[1152,128]{1,0:T(8,128)S(1)}) custom-call(f32[256,128]{1,0:T(8,128)S(1)} %shard_map.92.faces_ref.own_ref, f32[4096,128]{1,0:T(8,128)S(1)} %get-tuple-element.32.old_ref, ...), custom_call_target="tpu_custom_call", output_to_operand_aliasing={{0}: (1, {})} | custom-call | flops 8000000 | bytes 8000000 | tf_op jit(solution)/shard_map/pallas_call | solution.py:52
  67.2 0.0 collective-permute-done.12.refs_3_
  67.2 1.9 %collective-permute-done.11.refs_2_ = f32[256,128]{1,0:T(8,128)S(1)} collective-permute-done((f32[256,128]{1,0:T(8,128)S(1)}, f32[256,128]{1,0:T(8,128)S(1)}, u32[]{:S(2)}, u32[]{:S(2)}) %collective-permute-start.11) | collective-permute-done | bytes 131104 | tf_op jit(solution)/shard_map/ppermute | solution.py:375
  69.0 0.6 collective-permute-done.10.refs_1_
  69.7 0.0 collective-permute-done.9.refs_0_
  69.7 1.9 %shard_map.94 = f32[4096,128]{1,0:T(8,128)} custom-call(s32[6]{0:T(128)S(1)} %stack.23.scalar_ref, f32[256,128]{1,0:T(8,128)S(1)} %shard_map.92.faces_ref.own_ref, f32[256,128]{1,0:T(8,128)S(1)} %collective-permute-done.9.refs_0_, f32[256,128]{1,0:T(8,128)S(1)} %collective-permute-done.10.refs_1_, ...), custom_call_target="tpu_custom_call", output_to_operand_aliasing={{}: (10, {})} | custom-call | flops 1000000 | bytes 1000000 | tf_op jit(solution)/shard_map/pallas_call | solution.py:52
Async XLA Ops:
  0.6 19.3 %collective-permute-start = (bf16[4096,128]{1,0:T(8,128)(2,1)}, bf16[4096,128]{1,0:T(8,128)(2,1)S(1)}, u32[]{:S(2)}, u32[]{:S(2)}) collective-permute-start(bf16[4096,128]{1,0:T(8,128)(2,1)} %bitcast.18), channel_id=1, source_target_pairs={{0,1},{1,2},{2,3},{3,4},{4,5},{5,6},{6,7},{7,8},{8,9},{9,10},{10,1... | collective-permute-start | bytes 3145736 | tf_op jit(solution)/shard_map/ppermute | solution.py:391
  3.2 0.7 copy-start.5
  4.5 26.6 %all-to-all-start = ((s32[256,1,128]{2,1,0:T(1,128)}), s32[256,1,128]{2,1,0:T(1,128)S(1)}, u32[]{:S(2)}, u32[]{:S(2)}) async-start(s32[256,1,128]{2,1,0:T(1,128)} %bitcast.7), calls=%async_computation | async-start | bytes 262144 | tf_op jit(solution)/shard_map/all_to_all | solution.py:397
  21.5 0.8 %copy-start = (bf16[896,256]{1,0:T(8,128)(2,1)}, bf16[896,256]{1,0:T(8,128)(2,1)S(1)}, u32[]{:S(2)}) copy-start(bf16[896,256]{1,0:T(8,128)(2,1)S(1)} %get-tuple-element.20.staged_ref) | copy-start | bytes 1376260
  31.2 1.0 %copy-start.1 = (bf16[896,256]{1,0:T(8,128)(2,1)S(1)}, bf16[896,256]{1,0:T(8,128)(2,1)}, u32[]{:S(2)}) copy-start(bf16[896,256]{1,0:T(8,128)(2,1)} %copy-done) | copy-start | bytes 1376260
  33.2 9.6 %collective-permute-start.4 = (f32[256,128]{1,0:T(8,128)S(1)}, f32[256,128]{1,0:T(8,128)S(1)}, u32[]{:S(2)}, u32[]{:S(2)}) collective-permute-start(f32[256,128]{1,0:T(8,128)S(1)} %get-tuple-element.21.own_ref), channel_id=1, source_target_pairs={{1,2},{2,1},{3,4},{4,3},{5,6},{6,5},{7,8},{8,7},{9,10},{10,9},{11,... | collective-permute-start | bytes 393224 | tf_op jit(solution)/shard_map/ppermute | solution.py:375
  36.6 6.9 %collective-permute-start.3 = (f32[256,128]{1,0:T(8,128)S(1)}, f32[256,128]{1,0:T(8,128)S(1)}, u32[]{:S(2)}, u32[]{:S(2)}) collective-permute-start(f32[256,128]{1,0:T(8,128)S(1)} %get-tuple-element.21.own_ref), channel_id=1, source_target_pairs={{32,64},{64,32},{96,128},{128,96},{160,192},{192,160},{33,65},{65,... | collective-permute-start | bytes 393224 | tf_op jit(solution)/shard_map/ppermute | solution.py:375
  39.2 5.1 %collective-permute-start.2 = (f32[256,128]{1,0:T(8,128)S(1)}, f32[256,128]{1,0:T(8,128)S(1)}, u32[]{:S(2)}, u32[]{:S(2)}) collective-permute-start(f32[256,128]{1,0:T(8,128)S(1)} %get-tuple-element.21.own_ref), channel_id=1, source_target_pairs={{0,32},{32,0},{64,96},{96,64},{128,160},{160,128},{192,224},{224,1... | collective-permute-start | bytes 393224 | tf_op jit(solution)/shard_map/ppermute | solution.py:375
  39.3 5.0 %collective-permute-start.1 = (f32[256,128]{1,0:T(8,128)S(1)}, f32[256,128]{1,0:T(8,128)S(1)}, u32[]{:S(2)}, u32[]{:S(2)}) collective-permute-start(f32[256,128]{1,0:T(8,128)S(1)} %get-tuple-element.21.own_ref), channel_id=1, source_target_pairs={{0,1},{1,0},{2,3},{3,2},{4,5},{5,4},{6,7},{7,6},{8,9},{9,8},{10,11... | collective-permute-start | bytes 393224 | tf_op jit(solution)/shard_map/ppermute | solution.py:375
  39.4 4.9 %copy-start.2 = (s32[4,128]{1,0:T(4,128)S(1)}, s32[4,128]{1,0:T(4,128)}, u32[]{:S(2)}) copy-start(s32[4,128]{1,0:T(4,128)} %refs_4_.5) | copy-start | bytes 6148
  39.4 4.8 %copy-start.3 = (s32[4,128]{1,0:T(4,128)S(1)}, s32[4,128]{1,0:T(4,128)}, u32[]{:S(2)}) copy-start(s32[4,128]{1,0:T(4,128)} %refs_5_.5) | copy-start | bytes 6148
  39.5 4.8 %copy-start.4 = (s32[4,128]{1,0:T(4,128)S(1)}, s32[4,128]{1,0:T(4,128)}, u32[]{:S(2)}) copy-start(s32[4,128]{1,0:T(4,128)} %refs_6_.5) | copy-start | bytes 6148
  45.3 8.4 %collective-permute-start.8 = (f32[256,128]{1,0:T(8,128)S(1)}, f32[256,128]{1,0:T(8,128)S(1)}, u32[]{:S(2)}, u32[]{:S(2)}) collective-permute-start(f32[256,128]{1,0:T(8,128)S(1)} %shard_map.90.faces_ref.own_ref), channel_id=1, source_target_pairs={{1,2},{2,1},{3,4},{4,3},{5,6},{6,5},{7,8},{8,7},{9,10},{10,9},{11,... | collective-permute-start | bytes 393224 | tf_op jit(solution)/shard_map/ppermute | solution.py:375
  48.9 6.9 %collective-permute-start.7 = (f32[256,128]{1,0:T(8,128)S(1)}, f32[256,128]{1,0:T(8,128)S(1)}, u32[]{:S(2)}, u32[]{:S(2)}) collective-permute-start(f32[256,128]{1,0:T(8,128)S(1)} %shard_map.90.faces_ref.own_ref), channel_id=1, source_target_pairs={{32,64},{64,32},{96,128},{128,96},{160,192},{192,160},{33,65},{65,... | collective-permute-start | bytes 393224 | tf_op jit(solution)/shard_map/ppermute | solution.py:375
  52.4 5.1 %collective-permute-start.6 = (f32[256,128]{1,0:T(8,128)S(1)}, f32[256,128]{1,0:T(8,128)S(1)}, u32[]{:S(2)}, u32[]{:S(2)}) collective-permute-start(f32[256,128]{1,0:T(8,128)S(1)} %shard_map.90.faces_ref.own_ref), channel_id=1, source_target_pairs={{0,32},{32,0},{64,96},{96,64},{128,160},{160,128},{192,224},{224,1... | collective-permute-start | bytes 393224 | tf_op jit(solution)/shard_map/ppermute | solution.py:375
  52.5 5.0 %collective-permute-start.5 = (f32[256,128]{1,0:T(8,128)S(1)}, f32[256,128]{1,0:T(8,128)S(1)}, u32[]{:S(2)}, u32[]{:S(2)}) collective-permute-start(f32[256,128]{1,0:T(8,128)S(1)} %shard_map.90.faces_ref.own_ref), channel_id=1, source_target_pairs={{0,1},{1,0},{2,3},{3,2},{4,5},{5,4},{6,7},{7,6},{8,9},{9,8},{10,11... | collective-permute-start | bytes 393224 | tf_op jit(solution)/shard_map/ppermute | solution.py:375
  58.5 8.7 %collective-permute-start.12 = (f32[256,128]{1,0:T(8,128)S(1)}, f32[256,128]{1,0:T(8,128)S(1)}, u32[]{:S(2)}, u32[]{:S(2)}) collective-permute-start(f32[256,128]{1,0:T(8,128)S(1)} %shard_map.92.faces_ref.own_ref), channel_id=1, source_target_pairs={{1,2},{2,1},{3,4},{4,3},{5,6},{6,5},{7,8},{8,7},{9,10},{10,9},{11,... | collective-permute-start | bytes 393224 | tf_op jit(solution)/shard_map/ppermute | solution.py:375
  62.2 6.9 %collective-permute-start.11 = (f32[256,128]{1,0:T(8,128)S(1)}, f32[256,128]{1,0:T(8,128)S(1)}, u32[]{:S(2)}, u32[]{:S(2)}) collective-permute-start(f32[256,128]{1,0:T(8,128)S(1)} %shard_map.92.faces_ref.own_ref), channel_id=1, source_target_pairs={{32,64},{64,32},{96,128},{128,96},{160,192},{192,160},{33,65},{65,... | collective-permute-start | bytes 393224 | tf_op jit(solution)/shard_map/ppermute | solution.py:375
  64.6 5.1 %collective-permute-start.10 = (f32[256,128]{1,0:T(8,128)S(1)}, f32[256,128]{1,0:T(8,128)S(1)}, u32[]{:S(2)}, u32[]{:S(2)}) collective-permute-start(f32[256,128]{1,0:T(8,128)S(1)} %shard_map.92.faces_ref.own_ref), channel_id=1, source_target_pairs={{0,32},{32,0},{64,96},{96,64},{128,160},{160,128},{192,224},{224,1... | collective-permute-start | bytes 393224 | tf_op jit(solution)/shard_map/ppermute | solution.py:375
  64.7 5.0 %collective-permute-start.9 = (f32[256,128]{1,0:T(8,128)S(1)}, f32[256,128]{1,0:T(8,128)S(1)}, u32[]{:S(2)}, u32[]{:S(2)}) collective-permute-start(f32[256,128]{1,0:T(8,128)S(1)} %shard_map.92.faces_ref.own_ref), channel_id=1, source_target_pairs={{0,1},{1,0},{2,3},{3,2},{4,5},{5,4},{6,7},{7,6},{8,9},{9,8},{10,11... | collective-permute-start | bytes 393224 | tf_op jit(solution)/shard_map/ppermute | solution.py:375

commit v3 on v2

--- a/solution.py
+++ b/solution.py
@@ -22,13 +22,14 @@
 RHO_2 = 1.0 / (2.0 * SIGMA - RHO_1)
 C_1, K_1 = RHO_1 * RHO_0, 2.0 * RHO_1 / DELTA
 C_2, K_2 = RHO_2 * RHO_1, 2.0 * RHO_2 / DELTA
+SECOND = 1.0 + C_1 + K_1 * (THETA - 1.0)
 
 F32 = jnp.float32
 VMEM_LIMIT = 32 * 1024 * 1024
 
 
 def placed(array, space):
-    return array if space in (SMEM, ANY, FREE) else pltpu.with_memory_space_constraint(array, SPACES[space])
+    return array if space in (SMEM, ANY) else pltpu.with_memory_space_constraint(array, SPACES[space])
 
 
 def vmem(rows, dtype=F32):
@@ -43,8 +44,8 @@
     return pltpu.HBM(shape, F32)
 
 
-SMEM, VMEM, HBM, ANY, FREE = "smem", "vmem", "hbm", "any", "free"
-SPACES = {FREE: pltpu.VMEM, SMEM: pltpu.SMEM, VMEM: pltpu.VMEM, HBM: pltpu.HBM, ANY: pl.ANY}
+SMEM, VMEM, HBM, ANY = "smem", "vmem", "hbm", "any"
+SPACES = {SMEM: pltpu.SMEM, VMEM: pltpu.VMEM, HBM: pltpu.HBM, ANY: pl.ANY}
 
 
 def call(kernel, operands, outs, scratch=(), aliases=None, flops=1_000_000):
@@ -75,7 +76,13 @@
     out_ref[...] = jnp.broadcast_to(weight, out_ref.shape)
 
 
-def stage_kernel(prev_in, own_in, right_in, staged_ref, prev_ref, own_ref, wide_ref, edge_ref, faces_ref, sems):
+LINES_AT = ROWS
+RIGHT_AT = LINES_AT + 16 * B
+HELD = RIGHT_AT + 12 * B
+
+
+def stage_kernel(prev_in, own_in, right_in, prev_ref, held_ref, wide_ref, edge_ref, faces_ref, sems):
+    own_ref = held_ref.at[pl.ds(0, ROWS)]
     blocks = [
         pltpu.make_async_copy(of, to, sems.at[k])
         for k, (of, to) in enumerate(((prev_in, prev_ref), (own_in, own_ref)))
@@ -87,21 +94,23 @@
         reads.append(pltpu.make_async_copy(of, edge_ref.at[k], sems.at[4 + k]))
     for read in (*blocks, *reads):
         read.start()
-    for side, ref in enumerate((prev_ref, own_ref)):
+    for side, ref in enumerate((prev_ref, held_ref)):
         blocks[side].wait()
-        lanes = slice(side * LANES, (side + 1) * LANES)
-        wide_ref[...] = ref[...].astype(F32)
+        wide_ref[...] = ref[0:ROWS].astype(F32)
         for k, line in enumerate(LINES):
-            staged_ref[face(k), lanes] = ref[face(line)]
-            staged_ref[face(4 + k), lanes] = wide_ref[pl.ds(line, B, stride=B)].astype(jnp.bfloat16)
+            at = LINES_AT + (8 * side + k) * B
+            held_ref[at : at + B] = ref[face(line)]
+            at = at + 4 * B
+            held_ref[at : at + B] = wide_ref[pl.ds(line, B, stride=B)].astype(jnp.bfloat16)
     for read in reads:
         read.wait()
     for k in range(2):
         faces_ref[face(2 + k)] = edge_ref[k, :, 7 * k, :]
-    left = jnp.concatenate([faces_ref[0 : 2 * B], faces_ref[2 * B : 4 * B]], axis=1)
+    left = faces_ref[...]
     for piece in range(3):
         part = left.astype(jnp.bfloat16)
-        staged_ref[(8 + 2 * piece) * B : (10 + 2 * piece) * B] = part
+        at = RIGHT_AT + 4 * piece * B
+        held_ref[at : at + 4 * B] = part
         left = left - part.astype(F32)
 
 
@@ -137,13 +146,15 @@
     return one_hot, refined, first_bit, second_bit
 
 
-def face_kernel(scalar_ref, weights_ref, staged_ref, faces_ref, one_hot_ref, flags_ref, dup_ref):
+def face_kernel(scalar_ref, weights_ref, held_ref, faces_ref, one_hot_ref, flags_ref, dup_ref):
     one_hot, refined, first_bit, second_bit = lane_plan(scalar_ref[0], weights_ref)
     one_hot_ref[...] = one_hot
     flags_ref[...] = jnp.concatenate(
         [refined, first_bit, second_bit, jnp.zeros((5, LANES), F32)], axis=0
     )
-    lines = staged_ref[0 : 8 * B]
+    lines = jnp.concatenate(
+        [held_ref[LINES_AT : LINES_AT + 8 * B], held_ref[LINES_AT + 8 * B : RIGHT_AT]], axis=1
+    )
     picked = jnp.dot(lines, one_hot, preferred_element_type=F32)
     half = B // 2
     bits = (first_bit > 0.0, second_bit > 0.0)
@@ -157,13 +168,14 @@
         dup_ref[pl.ds(k * B, half, stride=2)] = chosen
         dup_ref[pl.ds(k * B + 1, half, stride=2)] = chosen
         coefficient = jnp.where(refined > 0.0, dup_ref[face(k)], plain)
-        lanes = slice((k // 2) * LANES, (k // 2 + 1) * LANES)
-        high, middle, low = (staged_ref[face(8 + 2 * i + k % 2), lanes].astype(F32) for i in range(3))
+        high, middle, low = (
+            held_ref[RIGHT_AT + (4 * i + k) * B : RIGHT_AT + (4 * i + k + 1) * B].astype(F32) for i in range(3)
+        )
         right = high + (middle + low)
         faces_ref[face(k)] = right / (4.0 + coefficient) * (1.0 / THETA)
 
 
-def sweep(field_ref, finish):
+def sweep(field_ref, finish, pieces=1, after=None):
     edge = lax.broadcasted_iota(jnp.int32, (B, LANES), 0)
     is_first, is_last = edge == 0, edge == B - 1
 
@@ -186,17 +198,21 @@
         total = total + jnp.where(is_first, 0.0, left) + jnp.where(is_last, 0.0, right)
         finish(at, centre, total)
 
-    plane(0, 0)
-
     def step(index, carry):
         plane(index, 1)
         return carry
 
-    lax.fori_loop(1, B - 1, step, 0, unroll=2)
-    plane(B - 1, 2)
-
-
-def build_kernel(prev_ref, own_ref, right_in, one_hot_ref, flags_ref, s_ref, inv_ref, diag_ref, part_ref, part_faces_ref, inv_faces_ref, right_ref, pick_ref, dup_ref, sem):
+    plane(0, 0)
+    bounds = [max(1, piece * B // pieces) for piece in range(pieces)] + [B - 1]
+    for piece in range(pieces):
+        lax.fori_loop(bounds[piece], bounds[piece + 1], step, 0, unroll=2)
+        if piece == pieces - 1:
+            plane(B - 1, 2)
+        if after is not None:
+            after(piece)
+
+
+def build_kernel(prev_ref, own_ref, right_in, one_hot_ref, flags_ref, s_ref, inv_ref, diag_ref, part_faces_ref, inv_faces_ref, right_ref, pick_ref, dup_ref, sem):
     read = pltpu.make_async_copy(right_in, right_ref, sem)
     read.start()
     chunk = ROWS // 8
@@ -233,50 +249,55 @@
 
     lax.fori_loop(0, half, leaf, 0, unroll=2)
 
-    def finish(at, centre, total):
-        part_ref[at] = (1.0 + C_1 + K_1 * (THETA - 1.0)) * centre + K_1 * (inv_ref[at] * total)
-
-    sweep(s_ref, finish)
+    edge = lax.broadcasted_iota(jnp.int32, (B, LANES), 0)
+    inside = (
+        s_ref[pl.ds(B, B)],
+        s_ref[pl.ds(ROWS - 2 * B, B)],
+        s_ref[pl.ds(1, B, stride=B)],
+        s_ref[pl.ds(B - 2, B, stride=B)],
+    )
     for k, at in enumerate(FACE_SLICES):
-        part_faces_ref[face(k)] = part_ref[at]
-        inv_faces_ref[face(k)] = inv_ref[at]
-
-
-def fill_ghosts(scalar_ref, source_refs, first_ref, second_ref, kind_ref, ghost_ref, pair_ref):
-    position = scalar_ref[0]
+        line, inv = s_ref[at], inv_ref[at]
+        total = inside[k] + jnp.where(edge == 0, 0.0, pltpu.roll(line, 1, 0))
+        total = total + jnp.where(edge == B - 1, 0.0, pltpu.roll(line, B - 1, 0))
+        part_faces_ref[face(k)] = SECOND * line + K_1 * (inv * total)
+        inv_faces_ref[face(k)] = inv
+
+
+def gathered(scalar_ref, index, side, source_refs):
+    offset = lax.shift_right_logical(index, 7) - scalar_ref[0]
+    lane = jnp.broadcast_to(index & (LANES - 1), (B, LANES))
+    value = jnp.zeros((B, LANES), F32)
+    for number, ref in enumerate(source_refs):
+        taken = jnp.take_along_axis(ref[face(side ^ 1)], lane, axis=1, mode="promise_in_bounds")
+        value = jnp.where(offset == scalar_ref[1 + number], taken, value)
+    return value
+
+
+def fill_ghost(side, scalar_ref, source_refs, first_ref, second_ref, kind_ref, ghost_ref, pair_ref):
     half = B // 2
-    for side in range(4):
-        kind = kind_ref[side : side + 1]
-        values = []
-        for index_ref in (first_ref, second_ref):
-            index = index_ref[side : side + 1]
-            offset = lax.shift_right_logical(index, 7) - position
-            lane = jnp.broadcast_to(index & (LANES - 1), (B, LANES))
-            value = jnp.zeros((B, LANES), F32)
-            for i, source_ref in enumerate(source_refs):
-                taken = jnp.take_along_axis(
-                    source_ref[face(side ^ 1)], lane, axis=1, mode="promise_in_bounds"
-                )
-                value = jnp.where(offset == scalar_ref[1 + i], taken, value)
-            values.append(value)
-        leading, second = values
-        at = side * 4 * B
-        pair_ref[at : at + B] = leading
-        pair_ref[at + B : at + 2 * B] = second
-        mean_low = (pair_ref[pl.ds(at, half, stride=2)] + pair_ref[pl.ds(at + 1, half, stride=2)]) * 0.5
-        mean_high = (
-            pair_ref[pl.ds(at + B, half, stride=2)] + pair_ref[pl.ds(at + B + 1, half, stride=2)]
-        ) * 0.5
-        for part in range(2):
-            for odd in range(2):
-                pair_ref[pl.ds(at + (2 + part) * B + odd, half, stride=2)] = leading[
-                    part * half : (part + 1) * half
-                ]
-        ghost = jnp.where(kind == 4, jnp.concatenate([mean_low, mean_high], axis=0), 0.0)
-        ghost = jnp.where(kind == 1, leading, ghost)
-        ghost = jnp.where(kind == 2, pair_ref[at + 2 * B : at + 3 * B], ghost)
-        ghost = jnp.where(kind == 3, pair_ref[at + 3 * B : at + 4 * B], ghost)
-        ghost_ref[face(side)] = ghost
+    kind = kind_ref[side : side + 1]
+    leading, second = (
+        gathered(scalar_ref, index_ref[side : side + 1], side, source_refs)
+        for index_ref in (first_ref, second_ref)
+    )
+    at = side * 4 * B
+    pair_ref[at : at + B] = leading
+    pair_ref[at + B : at + 2 * B] = second
+    mean_low = (pair_ref[pl.ds(at, half, stride=2)] + pair_ref[pl.ds(at + 1, half, stride=2)]) * 0.5
+    mean_high = (
+        pair_ref[pl.ds(at + B, half, stride=2)] + pair_ref[pl.ds(at + B + 1, half, stride=2)]
+    ) * 0.5
+    for part in range(2):
+        for odd in range(2):
+            pair_ref[pl.ds(at + (2 + part) * B + odd, half, stride=2)] = leading[
+                part * half : (part + 1) * half
+            ]
+    ghost = jnp.where(kind == 4, jnp.concatenate([mean_low, mean_high], axis=0), 0.0)
+    ghost = jnp.where(kind == 1, leading, ghost)
+    ghost = jnp.where(kind == 2, pair_ref[at + 2 * B : at + 3 * B], ghost)
+    ghost = jnp.where(kind == 3, pair_ref[at + 3 * B : at + 4 * B], ghost)
+    ghost_ref[face(side)] = ghost
 
 
 CORNERS = (
@@ -287,12 +308,10 @@
 )
 
 
-def step_faces_kernel(scale, scalar_ref, own_ref, *refs):
-    sources, (first_ref, second_ref, kind_ref, part_ref, inv_ref, out_ref, ghost_ref, sum_ref, pair_ref) = (
-        (own_ref, *refs[:4]),
-        refs[4:],
-    )
-    fill_ghosts(scalar_ref, sources, first_ref, second_ref, kind_ref, ghost_ref, pair_ref)
+def step_faces_kernel(scale, scalar_ref, *refs):
+    sources, plan, (part_ref, inv_ref, out_ref, ghost_ref, sum_ref, pair_ref) = refs[:5], refs[5:8], refs[8:]
+    for side in range(4):
+        fill_ghost(side, scalar_ref, sources, *plan, ghost_ref, pair_ref)
     sum_ref[...] = ghost_ref[...]
     for one, two in CORNERS:
         for (at_face, at_row), (of_face, of_row) in ((one, two), (two, one)):
@@ -301,7 +320,11 @@
     out_ref[...] = part_ref[...] + scale * (inv_ref[...] * sum_ref[...])
 
 
-def step_block_kernel(faces_ref, old_ref, u_ref, inv_ref, v_ref, part_ref, part_faces_ref):
+def step_block_kernel(faces_ref, u_ref, inv_ref, part_ref, part_faces_ref, v_ref):
+    def second(at, centre, total):
+        v_ref[at] = SECOND * centre + K_1 * (inv_ref[at] * total)
+
+    sweep(u_ref, second)
     for k, at in enumerate(FACE_SLICES):
         v_ref[at] = faces_ref[face(k)]
 
@@ -318,51 +341,52 @@
 def last_block_kernel(faces_ref, old_ref, right_ref, diag_ref, v_ref, out_ref, residual_ref, edge_ref, part_ref, sems):
     for k, at in enumerate(FACE_SLICES):
         v_ref[at] = faces_ref[face(k)]
-    write = pltpu.make_async_copy(v_ref, out_ref, sems.at[0])
-    write.start()
+    writes = [pltpu.make_async_copy(v_ref, out_ref, sems.at[0])]
+    writes[0].start()
 
     def finish(at, centre, total):
         part_ref[at] = right_ref[at] - diag_ref[at] * centre + total
 
-    sweep(v_ref, finish)
-    write_residual = pltpu.make_async_copy(part_ref, residual_ref, sems.at[1])
-    write_residual.start()
+    def write(quarter):
+        at = pl.ds(quarter * (ROWS // 4), ROWS // 4)
+        writes.append(pltpu.make_async_copy(part_ref.at[at], residual_ref.at[at], sems.at[1 + quarter]))
+        writes[-1].start()
+
+    sweep(v_ref, finish, 4, write)
     edge_ref[0:B] = part_ref[0:B]
     edge_ref[B : 2 * B] = part_ref[ROWS - B : ROWS]
     for plane in range(B):
         for k, tile in enumerate((0, B - 8)):
             to = 2 * B + k * 8 * B + plane * 8
             edge_ref[to : to + 8] = part_ref[plane * B + tile : plane * B + tile + 8]
-    write.wait()
-    write_residual.wait()
-
-
-def last_faces_kernel(scalar_ref, own_ref, *refs):
-    sources, refs = (own_ref, *refs[:4]), refs[4:]
-    first_ref, second_ref, kind_ref, edge_ref, _, out_ref, ghost_ref, pair_ref, sum_ref, sems = refs
-    fill_ghosts(scalar_ref, sources, first_ref, second_ref, kind_ref, ghost_ref, pair_ref)
-    sum_ref[...] = edge_ref[...]
-    sum_ref[0 : 2 * B] = sum_ref[0 : 2 * B] + ghost_ref[0 : 2 * B]
-    for (at_face, at_row), (of_face, of_row) in CORNERS:
-        at, of = at_face * B + at_row, of_face * B + of_row
-        sum_ref[at : at + 1] = sum_ref[at : at + 1] + ghost_ref[of : of + 1]
+    for copy in writes:
+        copy.wait()
+
+
+def last_faces_kernel(scalar_ref, *refs):
+    sources, plan, refs = (refs[0], *refs[2:5], refs[1]), refs[5:8], refs[8:]
+    edge_ref, _, out_ref, ghost_ref, pair_ref, sum_ref, sems = refs
     copies = []
+    cells = out_ref.reshape(B, B, LANES)
     for k in range(2):
         tiles = 2 * B + k * 8 * B
+        sum_ref[tiles : tiles + 8 * B] = edge_ref[tiles : tiles + 8 * B]
+        fill_ghost(2 + k, scalar_ref, sources, *plan, ghost_ref, pair_ref)
         at = pl.ds(tiles + 7 * k, B, stride=8)
         sum_ref[at] = sum_ref[at] + ghost_ref[face(2 + k)]
-        copies.append((face(k), pl.ds(k * (ROWS - B), B)))
-    copies = [
-        pltpu.make_async_copy(sum_ref.at[of], out_ref.at[to], sems.at[k]) for k, (of, to) in enumerate(copies)
-    ]
-    cells = out_ref.reshape(B, B, LANES)
+        of = sum_ref.at[pl.ds(tiles + 8, 8 * (B - 2))].reshape(B - 2, 8, LANES)
+        to = cells.at[pl.ds(1, B - 2), pl.ds(k * (B - 8), 8)]
+        copies.append(pltpu.make_async_copy(of, to, sems.at[2 + k]))
+        copies[-1].start()
     for k in range(2):
-        tiles = sum_ref.at[pl.ds(2 * B + k * 8 * B + 8, 8 * (B - 2))].reshape(B - 2, 8, LANES)
-        copies.append(
-            pltpu.make_async_copy(tiles, cells.at[pl.ds(1, B - 2), pl.ds(k * (B - 8), 8)], sems.at[2 + k])
-        )
-    for copy in copies:
-        copy.start()
+        fill_ghost(k, scalar_ref, sources, *plan, ghost_ref, pair_ref)
+        sum_ref[face(k)] = edge_ref[face(k)] + ghost_ref[face(k)]
+        for (at_face, at_row), (of_face, of_row) in CORNERS[2 * k : 2 * k + 2]:
+            at, of = at_face * B + at_row, of_face * B + of_row
+            sum_ref[at : at + 1] = sum_ref[at : at + 1] + ghost_ref[of : of + 1]
+        to = out_ref.at[pl.ds(k * (ROWS - B), B)]
+        copies.append(pltpu.make_async_copy(sum_ref.at[face(k)], to, sems.at[k]))
+        copies[-1].start()
     for copy in copies:
         copy.wait()
 
@@ -376,7 +400,7 @@
 
 
 def exchange(faces):
-    received = [swap(faces, "sfc", 0), swap(faces, "grp", 0), swap(faces, "grp", 1), swap(faces, "sfc", 1)]
+    received = [swap(faces, "sfc", 1), swap(faces, "grp", 1), swap(faces, "grp", 0), swap(faces, "sfc", 0)]
     return [(array, VMEM) for array in (faces, *received)]
 
 
@@ -386,36 +410,35 @@
     devices = lax.axis_size(AXES)
     position = grp * n_sfc + sfc
     right = right_side.reshape(ROWS, LANES)
-    flags = refine_flags.reshape(1, LANES)
     own = old_coef.reshape(ROWS, LANES)
     prev = lax.ppermute(own, AXES, [(i, i + 1) for i in range(devices - 1)])
     (spread,) = call(
         weights_kernel,
-        [(counts, SMEM), (flags, VMEM)],
+        [(counts, SMEM), (refine_flags.reshape(1, LANES), VMEM)],
         [(kept(devices, jnp.int32), VMEM)],
     )
     weights = lax.all_to_all(spread, AXES, 0, 0, tiled=True)
     even_sfc, even_grp = 1 - 2 * (sfc % 2), n_sfc * (1 - 2 * (grp % 2))
-    scalars = jnp.stack([position, 0, even_sfc, even_grp, -even_grp, -even_sfc]).astype(jnp.int32)
-
-    staged, prev, own = call(
+    scalars = jnp.stack([position, 0, -even_sfc, -even_grp, even_grp, even_sfc]).astype(jnp.int32)
+
+    prev, held = call(
         stage_kernel,
         [(prev, ANY), (own, HBM), (right_side, HBM)],
-        [(kept(14 * B, jnp.bfloat16, 2 * LANES), VMEM)] + [(kept(ROWS, jnp.bfloat16), VMEM)] * 2,
+        [(kept(ROWS, jnp.bfloat16), VMEM), (kept(HELD, jnp.bfloat16), VMEM)],
         [vmem(ROWS), pltpu.VMEM((2, B, 8, LANES), F32), vmem(4 * B), pltpu.SemaphoreType.DMA((6,))],
         flops=8_000_000,
     )
     faces, one_hot, flags = call(
         face_kernel,
-        [(scalars, SMEM), (weights, FREE), (staged, FREE)],
+        [(scalars, SMEM), (weights, VMEM), (held, VMEM)],
         [(kept(4 * B), VMEM), (kept(2 * LANES, jnp.bfloat16), VMEM), (kept(8), VMEM)],
         [vmem(4 * B)],
     )
     neighbours = exchange(faces)
-    s1, inv, diag, part, part_faces, inv_faces, right = call(
+    s1, inv, diag, part_faces, inv_faces, right = call(
         build_kernel,
-        [(prev, VMEM), (own, VMEM), (right, HBM), (one_hot, VMEM), (flags, VMEM)],
-        [(kept(ROWS), VMEM)] * 4 + [(kept(4 * B), VMEM)] * 2 + [(kept(ROWS), VMEM)],
+        [(prev, VMEM), (held, VMEM), (right, HBM), (one_hot, VMEM), (flags, VMEM)],
+        [(kept(ROWS), VMEM)] * 3 + [(kept(4 * B), VMEM)] * 2 + [(kept(ROWS), VMEM)],
         [vmem(ROWS), vmem(2 * B), pltpu.SemaphoreType.DMA],
         flops=8_000_000,
     )
@@ -428,11 +451,11 @@
         ghost_scratch,
     )
     neighbours = exchange(faces)
-    _, part, part_faces = call(
+    part, part_faces = call(
         step_block_kernel,
-        [(faces, VMEM), (part, VMEM), (s1, VMEM), (inv, VMEM)],
-        [(kept(ROWS), VMEM), (kept(ROWS), VMEM), (kept(4 * B), VMEM)],
-        aliases={1: 0},
+        [(faces, VMEM), (s1, VMEM), (inv, VMEM)],
+        [(kept(ROWS), VMEM), (kept(4 * B), VMEM)],
+        [vmem(ROWS)],
         flops=8_000_000,
     )
     (faces,) = call(
@@ -442,18 +465,20 @@
         ghost_scratch,
     )
     neighbours = exchange(faces)
+    neighbours = [neighbours[0], neighbours[4], *neighbours[1:4]]
+    whole = (in_hbm((ROWS, LANES)), HBM)
     _, iterate, residual, edges = call(
         last_block_kernel,
         [(faces, VMEM), (part, VMEM), (right, VMEM), (diag, VMEM)],
-        [(kept(ROWS), VMEM), (in_hbm((ROWS, LANES)), HBM), (in_hbm((ROWS, LANES)), HBM), (kept(18 * B), VMEM)],
-        [vmem(ROWS), pltpu.SemaphoreType.DMA((2,))],
+        [(kept(ROWS), VMEM), whole, whole, (kept(18 * B), VMEM)],
+        [vmem(ROWS), pltpu.SemaphoreType.DMA((5,))],
         aliases={1: 0},
         flops=8_000_000,
     )
     (residual,) = call(
         last_faces_kernel,
         [(scalars, SMEM), *neighbours, *plan, (edges, VMEM), (residual, HBM)],
-        [(in_hbm((ROWS, LANES)), HBM)],
+        [whole],
         [vmem(4 * B), vmem(16 * B), vmem(18 * B), pltpu.SemaphoreType.DMA((4,))],
         aliases={10: 0},
     )

time: 72 us -> 70.7 us (0.982)
  local copies, waits for them, and re-layouts: 2.53 us -> 1.72 us
    unnamed x12, local copies, waits for them, and re-layouts: 2.45 us -> 1.64 us
  transfers between devices with their start and end apart: 14 -> 14, of which waited for: 8 -> 7; matrix products, arithmetic and copies ran while one was open for 0% -> 0% of each run, Pallas kernels for 13% -> 13%
where the time goes in v3:
time: 70.7 us; the launch traced here: 70.4 us
  starting transfers between devices  36.8 us (52%)
  waiting for transfers between devices  16.5 us (23%)
  Pallas kernels  13.7 us (19%)
  local copies, waits for them, and re-layouts  1.72 us (2%)
  between operations  1.55 us (2%)
    ppermute x12, starting transfers between devices, swap(): return lax.ppermute(value, axis, pairs)  19.7 us
    all_to_all x1, starting transfers between devices, body(): weights = lax.all_to_all(spread, AXES, 0, 0, tiled=True)  15.2 us
    pallas_call x9, Pallas kernels, call(): pl.pallas_call(kernel, out_shape=[shape for shape, _ in outs], in_specs=s...  13.7 us
    all_to_all x1, waiting for transfers between devices, body(): weights = lax.all_to_all(spread, AXES, 0, 0, tiled=True)  8.69 us
    ppermute x12, waiting for transfers between devices, swap(): return lax.ppermute(value, axis, pairs)  7.83 us
    ppermute x1, starting transfers between devices, body(): prev = lax.ppermute(own, AXES, [(i, i + 1) for i in range(devices - 1)])  1.92 us
    unnamed x12, local copies, waits for them, and re-layouts  1.64 us
  transfers between devices with their start and end apart: 14, of which 7 were waited for; matrix products, arithmetic and copies ran while one was open for 0% of the time, Pallas kernels for 13%

profile of v3, /device:TPU:40, one launch (start us, length us, event | category | flops | bytes accessed | tf_op | source)
XLA Modules:
  0.0 70.4 jit_solution(16185394260495488763)
XLA Ops:
  0.6 1.9 %collective-permute-start = (bf16[4096,128]{1,0:T(8,128)(2,1)}, bf16[4096,128]{1,0:T(8,128)(2,1)S(1)}, u32[]{:S(2)}, u32[]{:S(2)}) collective-permute-start(bf16[4096,128]{1,0:T(8,128)(2,1)} %bitcast.18), channel_id=1, source_target_pairs={{0,1},{1,2},{2,3},{3,4},{4,5},{5,6},{6,7},{7,8},{8,9},{9,10},{10,1... | collective-permute-start | bytes 3145736 | tf_op jit(solution)/shard_map/ppermute | solution.py:414
  3.2 0.0 copy-start.5
  3.2 0.6 copy-done.5
  3.9 0.7 shard_map.86
  4.5 15.2 %all-to-all-start = ((s32[256,1,128]{2,1,0:T(1,128)}), s32[256,1,128]{2,1,0:T(1,128)S(1)}, u32[]{:S(2)}, u32[]{:S(2)}) async-start(s32[256,1,128]{2,1,0:T(1,128)} %bitcast.7), calls=%async_computation | async-start | bytes 262144 | tf_op jit(solution)/shard_map/all_to_all | solution.py:420
  19.8 0.1 stack.23.scalar_ref
  19.9 0.0 collective-permute-done.prev_in
  19.9 1.6 %shard_map.87 = (bf16[4096,128]{1,0:T(8,128)(2,1)S(1)}, bf16[5888,128]{1,0:T(8,128)(2,1)S(1)}) custom-call(bf16[4096,128]{1,0:T(8,128)(2,1)S(1)} %collective-permute-done.prev_in, bf16[4096,128]{1,0:T(8,128)(2,1)} %bitcast.19, f32[64,64,128]{2,1,0:T(8,128)} %right_in.1), custom_call_target="tpu_custom_call" | custom-call | flops 8000000 | bytes 8000000 | tf_op jit(solution)/shard_map/pallas_call | solution.py:53
  21.5 0.0 copy-start
  21.5 1.0 %copy-done = bf16[4096,128]{1,0:T(8,128)(2,1)} copy-done((bf16[4096,128]{1,0:T(8,128)(2,1)}, bf16[4096,128]{1,0:T(8,128)(2,1)S(1)}, u32[]{:S(2)}) %copy-start) | copy-done | bytes 1048600
  22.5 8.7 %all-to-all-done = s32[256,1,128]{2,1,0:T(1,128)S(1)} async-done(((s32[256,1,128]{2,1,0:T(1,128)}), s32[256,1,128]{2,1,0:T(1,128)S(1)}, u32[]{:S(2)}, u32[]{:S(2)}) %all-to-all-start) | async-done | bytes 131104 | tf_op jit(solution)/shard_map/all_to_all | solution.py:420
  31.2 0.0 copy-start.1
  31.2 1.1 %shard_map.88 = (f32[256,128]{1,0:T(8,128)S(1)}, bf16[256,128]{1,0:T(8,128)(2,1)S(1)}, f32[8,128]{1,0:T(8,128)S(1)}) custom-call(s32[6]{0:T(128)S(1)} %stack.23.scalar_ref, s32[256,128]{1,0:T(8,128)S(1)} %bitcast.14, bf16[5888,128]{1,0:T(8,128)(2,1)S(1)} %get-tuple-element.18.held_ref.own_ref), custom_call_target="tpu_custom_call" | custom-call | flops 1000000 | bytes 1000000 | tf_op jit(solution)/shard_map/pallas_call | solution.py:53
  32.2 3.3 %collective-permute-start.1 = (f32[256,128]{1,0:T(8,128)S(1)}, f32[256,128]{1,0:T(8,128)S(1)}, u32[]{:S(2)}, u32[]{:S(2)}) collective-permute-start(f32[256,128]{1,0:T(8,128)S(1)} %get-tuple-element.19.refs_0_), channel_id=1, source_target_pairs={{1,2},{2,1},{3,4},{4,3},{5,6},{6,5},{7,8},{8,7},{9,10},{10,9},{11,... | collective-permute-start | bytes 393224 | tf_op jit(solution)/shard_map/ppermute | solution.py:399
  35.6 2.6 %collective-permute-start.2 = (f32[256,128]{1,0:T(8,128)S(1)}, f32[256,128]{1,0:T(8,128)S(1)}, u32[]{:S(2)}, u32[]{:S(2)}) collective-permute-start(f32[256,128]{1,0:T(8,128)S(1)} %get-tuple-element.19.refs_0_), channel_id=1, source_target_pairs={{32,64},{64,32},{96,128},{128,96},{160,192},{192,160},{33,65},{65,... | collective-permute-start | bytes 393224 | tf_op jit(solution)/shard_map/ppermute | solution.py:399
  38.2 0.1 collective-permute-start.3
  38.3 0.1 collective-permute-start.4
  38.4 0.0 copy-done.1
  38.4 0.0 copy-start.2
  38.4 0.0 copy-start.3
  38.4 0.0 copy-start.4
  38.5 2.5 %shard_map.89 = (f32[4096,128]{1,0:T(8,128)S(1)}, f32[4096,128]{1,0:T(8,128)S(1)}, f32[4096,128]{1,0:T(8,128)S(1)}, f32[256,128]{1,0:T(8,128)S(1)}, f32[256,128]{1,0:T(8,128)S(1)}, /*index=5*/f32[4096,128]{1,0:T(8,128)S(1)}) custom-call(bf16[4096,128]{1,0:T(8,128)(2,1)S(1)} %copy-done.1, bf16[5888,128]{1,0:T(8,128)(2,1)S(1)} %get-tuple-element.18.held_ref.own_ref, ...), custom_call_target="tpu_custom_call" | custom-call | flops 8000000 | bytes 8000000 | tf_op jit(solution)/shard_map/pallas_call | solution.py:53
  41.0 0.0 collective-permute-done.1.refs_1_
  41.0 1.4 %collective-permute-done.2.refs_2_ = f32[256,128]{1,0:T(8,128)S(1)} collective-permute-done((f32[256,128]{1,0:T(8,128)S(1)}, f32[256,128]{1,0:T(8,128)S(1)}, u32[]{:S(2)}, u32[]{:S(2)}) %collective-permute-start.2) | collective-permute-done | bytes 131104 | tf_op jit(solution)/shard_map/ppermute | solution.py:399
  42.4 0.8 %collective-permute-done.3.refs_3_ = f32[256,128]{1,0:T(8,128)S(1)} collective-permute-done((f32[256,128]{1,0:T(8,128)S(1)}, f32[256,128]{1,0:T(8,128)S(1)}, u32[]{:S(2)}, u32[]{:S(2)}) %collective-permute-start.3) | collective-permute-done | bytes 131104 | tf_op jit(solution)/shard_map/ppermute | solution.py:399
  43.3 0.0 collective-permute-done.4.refs_4_
  43.3 0.0 copy-done.2
  43.3 0.0 copy-done.3
  43.3 0.0 copy-done.4
  43.3 1.0 %shard_map.90.faces_ref.refs_0_ = f32[256,128]{1,0:T(8,128)S(1)} custom-call(s32[6]{0:T(128)S(1)} %stack.23.scalar_ref, f32[256,128]{1,0:T(8,128)S(1)} %get-tuple-element.19.refs_0_, f32[256,128]{1,0:T(8,128)S(1)} %collective-permute-done.1.refs_1_, f32[256,128]{1,0:T(8,128)S(1)} %collective-permute-done.2.refs_2_, ...), custom_call_target="tpu_custom_call" | custom-call | flops 1000000 | bytes 1000000 | tf_op jit(solution)/shard_map/pallas_call | solution.py:53
  44.3 3.5 %collective-permute-start.5 = (f32[256,128]{1,0:T(8,128)S(1)}, f32[256,128]{1,0:T(8,128)S(1)}, u32[]{:S(2)}, u32[]{:S(2)}) collective-permute-start(f32[256,128]{1,0:T(8,128)S(1)} %shard_map.90.faces_ref.refs_0_), channel_id=1, source_target_pairs={{1,2},{2,1},{3,4},{4,3},{5,6},{6,5},{7,8},{8,7},{9,10},{10,9},{11,... | collective-permute-start | bytes 393224 | tf_op jit(solution)/shard_map/ppermute | solution.py:399
  47.8 3.5 %collective-permute-start.6 = (f32[256,128]{1,0:T(8,128)S(1)}, f32[256,128]{1,0:T(8,128)S(1)}, u32[]{:S(2)}, u32[]{:S(2)}) collective-permute-start(f32[256,128]{1,0:T(8,128)S(1)} %shard_map.90.faces_ref.refs_0_), channel_id=1, source_target_pairs={{32,64},{64,32},{96,128},{128,96},{160,192},{192,160},{33,65},{65,... | collective-permute-start | bytes 393224 | tf_op jit(solution)/shard_map/ppermute | solution.py:399
  51.3 0.1 collective-permute-start.7
  51.4 0.1 collective-permute-start.8
  51.5 2.0 %shard_map.91 = (f32[4096,128]{1,0:T(8,128)S(1)}, f32[256,128]{1,0:T(8,128)S(1)}) custom-call(f32[256,128]{1,0:T(8,128)S(1)} %shard_map.90.faces_ref.refs_0_, f32[4096,128]{1,0:T(8,128)S(1)} %get-tuple-element.25.u_ref, f32[4096,128]{1,0:T(8,128)S(1)} %get-tuple-element.26.inv_ref), custom_call_target="tpu_custom_call" | custom-call | flops 8000000 | bytes 8000000 | tf_op jit(solution)/shard_map/pallas_call | solution.py:53
  53.5 0.0 collective-permute-done.5.refs_1_
  53.5 1.2 %collective-permute-done.6.refs_2_ = f32[256,128]{1,0:T(8,128)S(1)} collective-permute-done((f32[256,128]{1,0:T(8,128)S(1)}, f32[256,128]{1,0:T(8,128)S(1)}, u32[]{:S(2)}, u32[]{:S(2)}) %collective-permute-start.6) | collective-permute-done | bytes 131104 | tf_op jit(solution)/shard_map/ppermute | solution.py:399
  54.7 1.7 %collective-permute-done.7.refs_3_ = f32[256,128]{1,0:T(8,128)S(1)} collective-permute-done((f32[256,128]{1,0:T(8,128)S(1)}, f32[256,128]{1,0:T(8,128)S(1)}, u32[]{:S(2)}, u32[]{:S(2)}) %collective-permute-start.7) | collective-permute-done | bytes 131104 | tf_op jit(solution)/shard_map/ppermute | solution.py:399
  56.4 0.0 collective-permute-done.8.refs_4_
  56.4 1.0 %shard_map.92.faces_ref.refs_0_ = f32[256,128]{1,0:T(8,128)S(1)} custom-call(s32[6]{0:T(128)S(1)} %stack.23.scalar_ref, f32[256,128]{1,0:T(8,128)S(1)} %shard_map.90.faces_ref.refs_0_, f32[256,128]{1,0:T(8,128)S(1)} %collective-permute-done.5.refs_1_, f32[256,128]{1,0:T(8,128)S(1)} %collective-permute-done.6.refs_2_, ...), custom_call_target="tpu_custom_call" | custom-call | flops 1000000 | bytes 1000000 | tf_op jit(solution)/shard_map/pallas_call | solution.py:53
  57.4 3.7 %collective-permute-start.10 = (f32[256,128]{1,0:T(8,128)S(1)}, f32[256,128]{1,0:T(8,128)S(1)}, u32[]{:S(2)}, u32[]{:S(2)}) collective-permute-start(f32[256,128]{1,0:T(8,128)S(1)} %shard_map.92.faces_ref.refs_0_), channel_id=1, source_target_pairs={{1,2},{2,1},{3,4},{4,3},{5,6},{6,5},{7,8},{8,7},{9,10},{10,9},{11,... | collective-permute-start | bytes 393224 | tf_op jit(solution)/shard_map/ppermute | solution.py:399
  61.2 2.4 %collective-permute-start.11 = (f32[256,128]{1,0:T(8,128)S(1)}, f32[256,128]{1,0:T(8,128)S(1)}, u32[]{:S(2)}, u32[]{:S(2)}) collective-permute-start(f32[256,128]{1,0:T(8,128)S(1)} %shard_map.92.faces_ref.refs_0_), channel_id=1, source_target_pairs={{32,64},{64,32},{96,128},{128,96},{160,192},{192,160},{33,65},{65,... | collective-permute-start | bytes 393224 | tf_op jit(solution)/shard_map/ppermute | solution.py:399
  63.6 0.1 collective-permute-start.12
  63.7 0.1 collective-permute-start.9
  63.8 2.1 %shard_map.93 = (f32[4096,128]{1,0:T(8,128)S(1)}, f32[4096,128]{1,0:T(8,128)}, f32[4096,128]{1,0:T(8,128)}, f32[1152,128]{1,0:T(8,128)S(1)}) custom-call(f32[256,128]{1,0:T(8,128)S(1)} %shard_map.92.faces_ref.refs_0_, f32[4096,128]{1,0:T(8,128)S(1)} %get-tuple-element.28.old_ref, ...), custom_call_target="tpu_custom_call", output_to_operand_aliasing={{0}: (1, {})} | custom-call | flops 8000000 | bytes 8000000 | tf_op jit(solution)/shard_map/pallas_call | solution.py:53
  65.9 0.0 collective-permute-done.10.refs_2_
  65.9 2.1 %collective-permute-done.11.refs_3_ = f32[256,128]{1,0:T(8,128)S(1)} collective-permute-done((f32[256,128]{1,0:T(8,128)S(1)}, f32[256,128]{1,0:T(8,128)S(1)}, u32[]{:S(2)}, u32[]{:S(2)}) %collective-permute-start.11) | collective-permute-done | bytes 131104 | tf_op jit(solution)/shard_map/ppermute | solution.py:399
  68.0 0.6 collective-permute-done.12.refs_4_
  68.7 0.0 collective-permute-done.9.refs_1_
  68.7 1.7 %shard_map.94 = f32[4096,128]{1,0:T(8,128)} custom-call(s32[6]{0:T(128)S(1)} %stack.23.scalar_ref, f32[256,128]{1,0:T(8,128)S(1)} %shard_map.92.faces_ref.refs_0_, f32[256,128]{1,0:T(8,128)S(1)} %collective-permute-done.9.refs_1_, f32[256,128]{1,0:T(8,128)S(1)} %collective-permute-done.10.refs_2_, ...), custom_call_target="tpu_custom_call", output_to_operand_aliasing={{}: (10, {})} | custom-call | flops 1000000 | bytes 1000000 | tf_op jit(solution)/shard_map/pallas_call | solution.py:53
Async XLA Ops:
  0.6 19.3 %collective-permute-start = (bf16[4096,128]{1,0:T(8,128)(2,1)}, bf16[4096,128]{1,0:T(8,128)(2,1)S(1)}, u32[]{:S(2)}, u32[]{:S(2)}) collective-permute-start(bf16[4096,128]{1,0:T(8,128)(2,1)} %bitcast.18), channel_id=1, source_target_pairs={{0,1},{1,2},{2,3},{3,4},{4,5},{5,6},{6,7},{7,8},{8,9},{9,10},{10,1... | collective-permute-start | bytes 3145736 | tf_op jit(solution)/shard_map/ppermute | solution.py:414
  3.2 0.7 copy-start.5
  4.5 26.6 %all-to-all-start = ((s32[256,1,128]{2,1,0:T(1,128)}), s32[256,1,128]{2,1,0:T(1,128)S(1)}, u32[]{:S(2)}, u32[]{:S(2)}) async-start(s32[256,1,128]{2,1,0:T(1,128)} %bitcast.7), calls=%async_computation | async-start | bytes 262144 | tf_op jit(solution)/shard_map/all_to_all | solution.py:420
  21.5 1.0 %copy-start = (bf16[4096,128]{1,0:T(8,128)(2,1)}, bf16[4096,128]{1,0:T(8,128)(2,1)S(1)}, u32[]{:S(2)}) copy-start(bf16[4096,128]{1,0:T(8,128)(2,1)S(1)} %get-tuple-element.20.prev_ref) | copy-start | bytes 3145732
  31.2 7.3 %copy-start.1 = (bf16[4096,128]{1,0:T(8,128)(2,1)S(1)}, bf16[4096,128]{1,0:T(8,128)(2,1)}, u32[]{:S(2)}) copy-start(bf16[4096,128]{1,0:T(8,128)(2,1)} %copy-done) | copy-start | bytes 3145732
  32.2 8.8 %collective-permute-start.1 = (f32[256,128]{1,0:T(8,128)S(1)}, f32[256,128]{1,0:T(8,128)S(1)}, u32[]{:S(2)}, u32[]{:S(2)}) collective-permute-start(f32[256,128]{1,0:T(8,128)S(1)} %get-tuple-element.19.refs_0_), channel_id=1, source_target_pairs={{1,2},{2,1},{3,4},{4,3},{5,6},{6,5},{7,8},{8,7},{9,10},{10,9},{11,... | collective-permute-start | bytes 393224 | tf_op jit(solution)/shard_map/ppermute | solution.py:399
  35.6 6.9 %collective-permute-start.2 = (f32[256,128]{1,0:T(8,128)S(1)}, f32[256,128]{1,0:T(8,128)S(1)}, u32[]{:S(2)}, u32[]{:S(2)}) collective-permute-start(f32[256,128]{1,0:T(8,128)S(1)} %get-tuple-element.19.refs_0_), channel_id=1, source_target_pairs={{32,64},{64,32},{96,128},{128,96},{160,192},{192,160},{33,65},{65,... | collective-permute-start | bytes 393224 | tf_op jit(solution)/shard_map/ppermute | solution.py:399
  38.2 5.1 %collective-permute-start.3 = (f32[256,128]{1,0:T(8,128)S(1)}, f32[256,128]{1,0:T(8,128)S(1)}, u32[]{:S(2)}, u32[]{:S(2)}) collective-permute-start(f32[256,128]{1,0:T(8,128)S(1)} %get-tuple-element.19.refs_0_), channel_id=1, source_target_pairs={{0,32},{32,0},{64,96},{96,64},{128,160},{160,128},{192,224},{224,1... | collective-permute-start | bytes 393224 | tf_op jit(solution)/shard_map/ppermute | solution.py:399
  38.3 5.0 %collective-permute-start.4 = (f32[256,128]{1,0:T(8,128)S(1)}, f32[256,128]{1,0:T(8,128)S(1)}, u32[]{:S(2)}, u32[]{:S(2)}) collective-permute-start(f32[256,128]{1,0:T(8,128)S(1)} %get-tuple-element.19.refs_0_), channel_id=1, source_target_pairs={{0,1},{1,0},{2,3},{3,2},{4,5},{5,4},{6,7},{7,6},{8,9},{9,8},{10,11... | collective-permute-start | bytes 393224 | tf_op jit(solution)/shard_map/ppermute | solution.py:399
  38.4 4.8 %copy-start.2 = (s32[4,128]{1,0:T(4,128)S(1)}, s32[4,128]{1,0:T(4,128)}, u32[]{:S(2)}) copy-start(s32[4,128]{1,0:T(4,128)} %refs_5_.5) | copy-start | bytes 6148
  38.4 4.8 %copy-start.3 = (s32[4,128]{1,0:T(4,128)S(1)}, s32[4,128]{1,0:T(4,128)}, u32[]{:S(2)}) copy-start(s32[4,128]{1,0:T(4,128)} %refs_6_.5) | copy-start | bytes 6148
  38.4 4.8 %copy-start.4 = (s32[4,128]{1,0:T(4,128)S(1)}, s32[4,128]{1,0:T(4,128)}, u32[]{:S(2)}) copy-start(s32[4,128]{1,0:T(4,128)} %refs_7_.5) | copy-start | bytes 6148
  44.3 9.2 %collective-permute-start.5 = (f32[256,128]{1,0:T(8,128)S(1)}, f32[256,128]{1,0:T(8,128)S(1)}, u32[]{:S(2)}, u32[]{:S(2)}) collective-permute-start(f32[256,128]{1,0:T(8,128)S(1)} %shard_map.90.faces_ref.refs_0_), channel_id=1, source_target_pairs={{1,2},{2,1},{3,4},{4,3},{5,6},{6,5},{7,8},{8,7},{9,10},{10,9},{11,... | collective-permute-start | bytes 393224 | tf_op jit(solution)/shard_map/ppermute | solution.py:399
  47.8 6.9 %collective-permute-start.6 = (f32[256,128]{1,0:T(8,128)S(1)}, f32[256,128]{1,0:T(8,128)S(1)}, u32[]{:S(2)}, u32[]{:S(2)}) collective-permute-start(f32[256,128]{1,0:T(8,128)S(1)} %shard_map.90.faces_ref.refs_0_), channel_id=1, source_target_pairs={{32,64},{64,32},{96,128},{128,96},{160,192},{192,160},{33,65},{65,... | collective-permute-start | bytes 393224 | tf_op jit(solution)/shard_map/ppermute | solution.py:399
  51.3 5.1 %collective-permute-start.7 = (f32[256,128]{1,0:T(8,128)S(1)}, f32[256,128]{1,0:T(8,128)S(1)}, u32[]{:S(2)}, u32[]{:S(2)}) collective-permute-start(f32[256,128]{1,0:T(8,128)S(1)} %shard_map.90.faces_ref.refs_0_), channel_id=1, source_target_pairs={{0,32},{32,0},{64,96},{96,64},{128,160},{160,128},{192,224},{224,1... | collective-permute-start | bytes 393224 | tf_op jit(solution)/shard_map/ppermute | solution.py:399
  51.4 5.0 %collective-permute-start.8 = (f32[256,128]{1,0:T(8,128)S(1)}, f32[256,128]{1,0:T(8,128)S(1)}, u32[]{:S(2)}, u32[]{:S(2)}) collective-permute-start(f32[256,128]{1,0:T(8,128)S(1)} %shard_map.90.faces_ref.refs_0_), channel_id=1, source_target_pairs={{0,1},{1,0},{2,3},{3,2},{4,5},{5,4},{6,7},{7,6},{8,9},{9,8},{10,11... | collective-permute-start | bytes 393224 | tf_op jit(solution)/shard_map/ppermute | solution.py:399
  57.4 8.5 %collective-permute-start.10 = (f32[256,128]{1,0:T(8,128)S(1)}, f32[256,128]{1,0:T(8,128)S(1)}, u32[]{:S(2)}, u32[]{:S(2)}) collective-permute-start(f32[256,128]{1,0:T(8,128)S(1)} %shard_map.92.faces_ref.refs_0_), channel_id=1, source_target_pairs={{1,2},{2,1},{3,4},{4,3},{5,6},{6,5},{7,8},{8,7},{9,10},{10,9},{11,... | collective-permute-start | bytes 393224 | tf_op jit(solution)/shard_map/ppermute | solution.py:399
  61.2 6.9 %collective-permute-start.11 = (f32[256,128]{1,0:T(8,128)S(1)}, f32[256,128]{1,0:T(8,128)S(1)}, u32[]{:S(2)}, u32[]{:S(2)}) collective-permute-start(f32[256,128]{1,0:T(8,128)S(1)} %shard_map.92.faces_ref.refs_0_), channel_id=1, source_target_pairs={{32,64},{64,32},{96,128},{128,96},{160,192},{192,160},{33,65},{65,... | collective-permute-start | bytes 393224 | tf_op jit(solution)/shard_map/ppermute | solution.py:399
  63.6 5.1 %collective-permute-start.12 = (f32[256,128]{1,0:T(8,128)S(1)}, f32[256,128]{1,0:T(8,128)S(1)}, u32[]{:S(2)}, u32[]{:S(2)}) collective-permute-start(f32[256,128]{1,0:T(8,128)S(1)} %shard_map.92.faces_ref.refs_0_), channel_id=1, source_target_pairs={{0,32},{32,0},{64,96},{96,64},{128,160},{160,128},{192,224},{224,1... | collective-permute-start | bytes 393224 | tf_op jit(solution)/shard_map/ppermute | solution.py:399
  63.7 5.0 %collective-permute-start.9 = (f32[256,128]{1,0:T(8,128)S(1)}, f32[256,128]{1,0:T(8,128)S(1)}, u32[]{:S(2)}, u32[]{:S(2)}) collective-permute-start(f32[256,128]{1,0:T(8,128)S(1)} %shard_map.92.faces_ref.refs_0_), channel_id=1, source_target_pairs={{0,1},{1,0},{2,3},{3,2},{4,5},{5,4},{6,7},{7,6},{8,9},{9,8},{10,11... | collective-permute-start | bytes 393224 | tf_op jit(solution)/shard_map/ppermute | solution.py:399

commit v4 on v3

--- a/solution.py
+++ b/solution.py
@@ -400,7 +400,7 @@
 
 
 def exchange(faces):
-    received = [swap(faces, "sfc", 1), swap(faces, "grp", 1), swap(faces, "grp", 0), swap(faces, "sfc", 0)]
+    received = [swap(faces, "grp", 1), swap(faces, "sfc", 1), swap(faces, "grp", 0), swap(faces, "sfc", 0)]
     return [(array, VMEM) for array in (faces, *received)]
 
 
@@ -419,7 +419,7 @@
     )
     weights = lax.all_to_all(spread, AXES, 0, 0, tiled=True)
     even_sfc, even_grp = 1 - 2 * (sfc % 2), n_sfc * (1 - 2 * (grp % 2))
-    scalars = jnp.stack([position, 0, -even_sfc, -even_grp, even_grp, even_sfc]).astype(jnp.int32)
+    scalars = jnp.stack([position, 0, -even_grp, -even_sfc, even_grp, even_sfc]).astype(jnp.int32)
 
     prev, held = call(
         stage_kernel,

time: 70.7 us -> 70.3 us (level)
  starting transfers between devices: 36.8 us -> 35.7 us
    ppermute x12, starting transfers between devices: 19.7 us -> 18.6 us  [swap(): return lax.ppermute(value, axis, pairs)]
  transfers between devices with their start and end apart: 14 -> 14, of which waited for: 7 -> 5; matrix products, arithmetic and copies ran while one was open for 0% -> 0% of each run, Pallas kernels for 13% -> 13%
where the time goes in v4:
time: 70.3 us; the launch traced here: 69.9 us
  starting transfers between devices  35.7 us (51%)
  waiting for transfers between devices  17.2 us (24%)
  Pallas kernels  13.7 us (19%)
  local copies, waits for them, and re-layouts  1.72 us (2%)
  between operations  1.56 us (2%)
    ppermute x12, starting transfers between devices, swap(): return lax.ppermute(value, axis, pairs)  18.6 us
    all_to_all x1, starting transfers between devices, body(): weights = lax.all_to_all(spread, AXES, 0, 0, tiled=True)  15.2 us
    pallas_call x9, Pallas kernels, call(): pl.pallas_call(kernel, out_shape=[shape for shape, _ in outs], in_specs=s...  13.7 us
    all_to_all x1, waiting for transfers between devices, body(): weights = lax.all_to_all(spread, AXES, 0, 0, tiled=True)  8.69 us
    ppermute x12, waiting for transfers between devices, swap(): return lax.ppermute(value, axis, pairs)  8.5 us
    ppermute x1, starting transfers between devices, body(): prev = lax.ppermute(own, AXES, [(i, i + 1) for i in range(devices - 1)])  1.92 us
    unnamed x12, local copies, waits for them, and re-layouts  1.64 us
  transfers between devices with their start and end apart: 14, of which 5 were waited for; matrix products, arithmetic and copies ran while one was open for 0% of the time, Pallas kernels for 13%

profile of v4, /device:TPU:40, one launch (start us, length us, event | category | flops | bytes accessed | tf_op | source)
XLA Modules:
  0.0 69.9 jit_solution(17320801047739771785)
XLA Ops:
  0.6 1.9 %collective-permute-start = (bf16[4096,128]{1,0:T(8,128)(2,1)}, bf16[4096,128]{1,0:T(8,128)(2,1)S(1)}, u32[]{:S(2)}, u32[]{:S(2)}) collective-permute-start(bf16[4096,128]{1,0:T(8,128)(2,1)} %bitcast.18), channel_id=1, source_target_pairs={{0,1},{1,2},{2,3},{3,4},{4,5},{5,6},{6,7},{7,8},{8,9},{9,10},{10,1... | collective-permute-start | bytes 3145736 | tf_op jit(solution)/shard_map/ppermute | solution.py:414
  3.2 0.0 copy-start.5
  3.2 0.6 copy-done.5
  3.9 0.7 shard_map.86
  4.5 15.2 %all-to-all-start = ((s32[256,1,128]{2,1,0:T(1,128)}), s32[256,1,128]{2,1,0:T(1,128)S(1)}, u32[]{:S(2)}, u32[]{:S(2)}) async-start(s32[256,1,128]{2,1,0:T(1,128)} %bitcast.7), calls=%async_computation | async-start | bytes 262144 | tf_op jit(solution)/shard_map/all_to_all | solution.py:420
  19.8 0.1 stack.23.scalar_ref
  19.9 0.0 collective-permute-done.prev_in
  19.9 1.6 %shard_map.87 = (bf16[4096,128]{1,0:T(8,128)(2,1)S(1)}, bf16[5888,128]{1,0:T(8,128)(2,1)S(1)}) custom-call(bf16[4096,128]{1,0:T(8,128)(2,1)S(1)} %collective-permute-done.prev_in, bf16[4096,128]{1,0:T(8,128)(2,1)} %bitcast.19, f32[64,64,128]{2,1,0:T(8,128)} %right_in.1), custom_call_target="tpu_custom_call" | custom-call | flops 8000000 | bytes 8000000 | tf_op jit(solution)/shard_map/pallas_call | solution.py:53
  21.5 0.0 copy-start
  21.5 1.0 %copy-done = bf16[4096,128]{1,0:T(8,128)(2,1)} copy-done((bf16[4096,128]{1,0:T(8,128)(2,1)}, bf16[4096,128]{1,0:T(8,128)(2,1)S(1)}, u32[]{:S(2)}) %copy-start) | copy-done | bytes 1048600
  22.5 8.7 %all-to-all-done = s32[256,1,128]{2,1,0:T(1,128)S(1)} async-done(((s32[256,1,128]{2,1,0:T(1,128)}), s32[256,1,128]{2,1,0:T(1,128)S(1)}, u32[]{:S(2)}, u32[]{:S(2)}) %all-to-all-start) | async-done | bytes 131104 | tf_op jit(solution)/shard_map/all_to_all | solution.py:420
  31.2 0.0 copy-start.1
  31.2 1.1 %shard_map.88 = (f32[256,128]{1,0:T(8,128)S(1)}, bf16[256,128]{1,0:T(8,128)(2,1)S(1)}, f32[8,128]{1,0:T(8,128)S(1)}) custom-call(s32[6]{0:T(128)S(1)} %stack.23.scalar_ref, s32[256,128]{1,0:T(8,128)S(1)} %bitcast.14, bf16[5888,128]{1,0:T(8,128)(2,1)S(1)} %get-tuple-element.18.held_ref.own_ref), custom_call_target="tpu_custom_call" | custom-call | flops 1000000 | bytes 1000000 | tf_op jit(solution)/shard_map/pallas_call | solution.py:53
  32.2 2.8 %collective-permute-start.1 = (f32[256,128]{1,0:T(8,128)S(1)}, f32[256,128]{1,0:T(8,128)S(1)}, u32[]{:S(2)}, u32[]{:S(2)}) collective-permute-start(f32[256,128]{1,0:T(8,128)S(1)} %get-tuple-element.19.refs_0_), channel_id=1, source_target_pairs={{32,64},{64,32},{96,128},{128,96},{160,192},{192,160},{33,65},{65,... | collective-permute-start | bytes 393224 | tf_op jit(solution)/shard_map/ppermute | solution.py:399
  35.0 2.9 %collective-permute-start.2 = (f32[256,128]{1,0:T(8,128)S(1)}, f32[256,128]{1,0:T(8,128)S(1)}, u32[]{:S(2)}, u32[]{:S(2)}) collective-permute-start(f32[256,128]{1,0:T(8,128)S(1)} %get-tuple-element.19.refs_0_), channel_id=1, source_target_pairs={{1,2},{2,1},{3,4},{4,3},{5,6},{6,5},{7,8},{8,7},{9,10},{10,9},{11,... | collective-permute-start | bytes 393224 | tf_op jit(solution)/shard_map/ppermute | solution.py:399
  37.9 0.1 collective-permute-start.3
  38.0 0.1 collective-permute-start.4
  38.1 0.0 copy-done.1
  38.1 0.0 copy-start.2
  38.2 0.0 copy-start.3
  38.2 0.0 copy-start.4
  38.2 2.5 %shard_map.89 = (f32[4096,128]{1,0:T(8,128)S(1)}, f32[4096,128]{1,0:T(8,128)S(1)}, f32[4096,128]{1,0:T(8,128)S(1)}, f32[256,128]{1,0:T(8,128)S(1)}, f32[256,128]{1,0:T(8,128)S(1)}, /*index=5*/f32[4096,128]{1,0:T(8,128)S(1)}) custom-call(bf16[4096,128]{1,0:T(8,128)(2,1)S(1)} %copy-done.1, bf16[5888,128]{1,0:T(8,128)(2,1)S(1)} %get-tuple-element.18.held_ref.own_ref, ...), custom_call_target="tpu_custom_call" | custom-call | flops 8000000 | bytes 8000000 | tf_op jit(solution)/shard_map/pallas_call | solution.py:53
  40.7 0.0 collective-permute-done.1.refs_1_
  40.7 2.7 %collective-permute-done.2.refs_2_ = f32[256,128]{1,0:T(8,128)S(1)} collective-permute-done((f32[256,128]{1,0:T(8,128)S(1)}, f32[256,128]{1,0:T(8,128)S(1)}, u32[]{:S(2)}, u32[]{:S(2)}) %collective-permute-start.2) | collective-permute-done | bytes 131104 | tf_op jit(solution)/shard_map/ppermute | solution.py:399
  43.4 0.0 collective-permute-done.3.refs_3_
  43.4 0.0 collective-permute-done.4.refs_4_
  43.4 0.0 copy-done.2
  43.4 0.0 copy-done.3
  43.5 0.0 copy-done.4
  43.5 1.0 %shard_map.90.faces_ref.refs_0_ = f32[256,128]{1,0:T(8,128)S(1)} custom-call(s32[6]{0:T(128)S(1)} %stack.23.scalar_ref, f32[256,128]{1,0:T(8,128)S(1)} %get-tuple-element.19.refs_0_, f32[256,128]{1,0:T(8,128)S(1)} %collective-permute-done.1.refs_1_, f32[256,128]{1,0:T(8,128)S(1)} %collective-permute-done.2.refs_2_, ...), custom_call_target="tpu_custom_call" | custom-call | flops 1000000 | bytes 1000000 | tf_op jit(solution)/shard_map/pallas_call | solution.py:53
  44.5 3.0 %collective-permute-start.5 = (f32[256,128]{1,0:T(8,128)S(1)}, f32[256,128]{1,0:T(8,128)S(1)}, u32[]{:S(2)}, u32[]{:S(2)}) collective-permute-start(f32[256,128]{1,0:T(8,128)S(1)} %shard_map.90.faces_ref.refs_0_), channel_id=1, source_target_pairs={{32,64},{64,32},{96,128},{128,96},{160,192},{192,160},{33,65},{65,... | collective-permute-start | bytes 393224 | tf_op jit(solution)/shard_map/ppermute | solution.py:399
  47.6 3.5 %collective-permute-start.6 = (f32[256,128]{1,0:T(8,128)S(1)}, f32[256,128]{1,0:T(8,128)S(1)}, u32[]{:S(2)}, u32[]{:S(2)}) collective-permute-start(f32[256,128]{1,0:T(8,128)S(1)} %shard_map.90.faces_ref.refs_0_), channel_id=1, source_target_pairs={{1,2},{2,1},{3,4},{4,3},{5,6},{6,5},{7,8},{8,7},{9,10},{10,9},{11,... | collective-permute-start | bytes 393224 | tf_op jit(solution)/shard_map/ppermute | solution.py:399
  51.1 0.1 collective-permute-start.7
  51.2 0.1 collective-permute-start.8
  51.3 2.0 %shard_map.91 = (f32[4096,128]{1,0:T(8,128)S(1)}, f32[256,128]{1,0:T(8,128)S(1)}) custom-call(f32[256,128]{1,0:T(8,128)S(1)} %shard_map.90.faces_ref.refs_0_, f32[4096,128]{1,0:T(8,128)S(1)} %get-tuple-element.25.u_ref, f32[4096,128]{1,0:T(8,128)S(1)} %get-tuple-element.26.inv_ref), custom_call_target="tpu_custom_call" | custom-call | flops 8000000 | bytes 8000000 | tf_op jit(solution)/shard_map/pallas_call | solution.py:53
  53.3 0.0 collective-permute-done.5.refs_1_
  53.3 2.7 %collective-permute-done.6.refs_2_ = f32[256,128]{1,0:T(8,128)S(1)} collective-permute-done((f32[256,128]{1,0:T(8,128)S(1)}, f32[256,128]{1,0:T(8,128)S(1)}, u32[]{:S(2)}, u32[]{:S(2)}) %collective-permute-start.6) | collective-permute-done | bytes 131104 | tf_op jit(solution)/shard_map/ppermute | solution.py:399
  55.9 0.2 collective-permute-done.7.refs_3_
  56.1 0.0 collective-permute-done.8.refs_4_
  56.1 1.0 %shard_map.92.faces_ref.refs_0_ = f32[256,128]{1,0:T(8,128)S(1)} custom-call(s32[6]{0:T(128)S(1)} %stack.23.scalar_ref, f32[256,128]{1,0:T(8,128)S(1)} %shard_map.90.faces_ref.refs_0_, f32[256,128]{1,0:T(8,128)S(1)} %collective-permute-done.5.refs_1_, f32[256,128]{1,0:T(8,128)S(1)} %collective-permute-done.6.refs_2_, ...), custom_call_target="tpu_custom_call" | custom-call | flops 1000000 | bytes 1000000 | tf_op jit(solution)/shard_map/pallas_call | solution.py:53
  57.2 2.6 %collective-permute-start.10 = (f32[256,128]{1,0:T(8,128)S(1)}, f32[256,128]{1,0:T(8,128)S(1)}, u32[]{:S(2)}, u32[]{:S(2)}) collective-permute-start(f32[256,128]{1,0:T(8,128)S(1)} %shard_map.92.faces_ref.refs_0_), channel_id=1, source_target_pairs={{32,64},{64,32},{96,128},{128,96},{160,192},{192,160},{33,65},{65,... | collective-permute-start | bytes 393224 | tf_op jit(solution)/shard_map/ppermute | solution.py:399
  59.8 3.1 %collective-permute-start.11 = (f32[256,128]{1,0:T(8,128)S(1)}, f32[256,128]{1,0:T(8,128)S(1)}, u32[]{:S(2)}, u32[]{:S(2)}) collective-permute-start(f32[256,128]{1,0:T(8,128)S(1)} %shard_map.92.faces_ref.refs_0_), channel_id=1, source_target_pairs={{1,2},{2,1},{3,4},{4,3},{5,6},{6,5},{7,8},{8,7},{9,10},{10,9},{11,... | collective-permute-start | bytes 393224 | tf_op jit(solution)/shard_map/ppermute | solution.py:399
  62.9 0.1 collective-permute-start.12
  63.0 0.1 collective-permute-start.9
  63.1 2.1 %shard_map.93 = (f32[4096,128]{1,0:T(8,128)S(1)}, f32[4096,128]{1,0:T(8,128)}, f32[4096,128]{1,0:T(8,128)}, f32[1152,128]{1,0:T(8,128)S(1)}) custom-call(f32[256,128]{1,0:T(8,128)S(1)} %shard_map.92.faces_ref.refs_0_, f32[4096,128]{1,0:T(8,128)S(1)} %get-tuple-element.28.old_ref, ...), custom_call_target="tpu_custom_call", output_to_operand_aliasing={{0}: (1, {})} | custom-call | flops 8000000 | bytes 8000000 | tf_op jit(solution)/shard_map/pallas_call | solution.py:53
  65.3 0.0 collective-permute-done.10.refs_2_
  65.3 2.9 %collective-permute-done.11.refs_3_ = f32[256,128]{1,0:T(8,128)S(1)} collective-permute-done((f32[256,128]{1,0:T(8,128)S(1)}, f32[256,128]{1,0:T(8,128)S(1)}, u32[]{:S(2)}, u32[]{:S(2)}) %collective-permute-start.11) | collective-permute-done | bytes 131104 | tf_op jit(solution)/shard_map/ppermute | solution.py:399
  68.2 0.0 collective-permute-done.12.refs_4_
  68.2 0.0 collective-permute-done.9.refs_1_
  68.2 1.7 %shard_map.94 = f32[4096,128]{1,0:T(8,128)} custom-call(s32[6]{0:T(128)S(1)} %stack.23.scalar_ref, f32[256,128]{1,0:T(8,128)S(1)} %shard_map.92.faces_ref.refs_0_, f32[256,128]{1,0:T(8,128)S(1)} %collective-permute-done.9.refs_1_, f32[256,128]{1,0:T(8,128)S(1)} %collective-permute-done.10.refs_2_, ...), custom_call_target="tpu_custom_call", output_to_operand_aliasing={{}: (10, {})} | custom-call | flops 1000000 | bytes 1000000 | tf_op jit(solution)/shard_map/pallas_call | solution.py:53
Async XLA Ops:
  0.6 19.3 %collective-permute-start = (bf16[4096,128]{1,0:T(8,128)(2,1)}, bf16[4096,128]{1,0:T(8,128)(2,1)S(1)}, u32[]{:S(2)}, u32[]{:S(2)}) collective-permute-start(bf16[4096,128]{1,0:T(8,128)(2,1)} %bitcast.18), channel_id=1, source_target_pairs={{0,1},{1,2},{2,3},{3,4},{4,5},{5,6},{6,7},{7,8},{8,9},{9,10},{10,1... | collective-permute-start | bytes 3145736 | tf_op jit(solution)/shard_map/ppermute | solution.py:414
  3.2 0.7 copy-start.5
  4.5 26.6 %all-to-all-start = ((s32[256,1,128]{2,1,0:T(1,128)}), s32[256,1,128]{2,1,0:T(1,128)S(1)}, u32[]{:S(2)}, u32[]{:S(2)}) async-start(s32[256,1,128]{2,1,0:T(1,128)} %bitcast.7), calls=%async_computation | async-start | bytes 262144 | tf_op jit(solution)/shard_map/all_to_all | solution.py:420
  21.5 1.0 %copy-start = (bf16[4096,128]{1,0:T(8,128)(2,1)}, bf16[4096,128]{1,0:T(8,128)(2,1)S(1)}, u32[]{:S(2)}) copy-start(bf16[4096,128]{1,0:T(8,128)(2,1)S(1)} %get-tuple-element.20.prev_ref) | copy-start | bytes 3145732
  31.2 7.0 %copy-start.1 = (bf16[4096,128]{1,0:T(8,128)(2,1)S(1)}, bf16[4096,128]{1,0:T(8,128)(2,1)}, u32[]{:S(2)}) copy-start(bf16[4096,128]{1,0:T(8,128)(2,1)} %copy-done) | copy-start | bytes 3145732
  32.2 8.5 %collective-permute-start.1 = (f32[256,128]{1,0:T(8,128)S(1)}, f32[256,128]{1,0:T(8,128)S(1)}, u32[]{:S(2)}, u32[]{:S(2)}) collective-permute-start(f32[256,128]{1,0:T(8,128)S(1)} %get-tuple-element.19.refs_0_), channel_id=1, source_target_pairs={{32,64},{64,32},{96,128},{128,96},{160,192},{192,160},{33,65},{65,... | collective-permute-start | bytes 393224 | tf_op jit(solution)/shard_map/ppermute | solution.py:399
  35.0 8.4 %collective-permute-start.2 = (f32[256,128]{1,0:T(8,128)S(1)}, f32[256,128]{1,0:T(8,128)S(1)}, u32[]{:S(2)}, u32[]{:S(2)}) collective-permute-start(f32[256,128]{1,0:T(8,128)S(1)} %get-tuple-element.19.refs_0_), channel_id=1, source_target_pairs={{1,2},{2,1},{3,4},{4,3},{5,6},{6,5},{7,8},{8,7},{9,10},{10,9},{11,... | collective-permute-start | bytes 393224 | tf_op jit(solution)/shard_map/ppermute | solution.py:399
  37.9 5.5 %collective-permute-start.3 = (f32[256,128]{1,0:T(8,128)S(1)}, f32[256,128]{1,0:T(8,128)S(1)}, u32[]{:S(2)}, u32[]{:S(2)}) collective-permute-start(f32[256,128]{1,0:T(8,128)S(1)} %get-tuple-element.19.refs_0_), channel_id=1, source_target_pairs={{0,32},{32,0},{64,96},{96,64},{128,160},{160,128},{192,224},{224,1... | collective-permute-start | bytes 393224 | tf_op jit(solution)/shard_map/ppermute | solution.py:399
  38.0 5.4 %collective-permute-start.4 = (f32[256,128]{1,0:T(8,128)S(1)}, f32[256,128]{1,0:T(8,128)S(1)}, u32[]{:S(2)}, u32[]{:S(2)}) collective-permute-start(f32[256,128]{1,0:T(8,128)S(1)} %get-tuple-element.19.refs_0_), channel_id=1, source_target_pairs={{0,1},{1,0},{2,3},{3,2},{4,5},{5,4},{6,7},{7,6},{8,9},{9,8},{10,11... | collective-permute-start | bytes 393224 | tf_op jit(solution)/shard_map/ppermute | solution.py:399
  38.1 5.3 %copy-start.2 = (s32[4,128]{1,0:T(4,128)S(1)}, s32[4,128]{1,0:T(4,128)}, u32[]{:S(2)}) copy-start(s32[4,128]{1,0:T(4,128)} %refs_5_.5) | copy-start | bytes 6148
  38.2 5.3 %copy-start.3 = (s32[4,128]{1,0:T(4,128)S(1)}, s32[4,128]{1,0:T(4,128)}, u32[]{:S(2)}) copy-start(s32[4,128]{1,0:T(4,128)} %refs_6_.5) | copy-start | bytes 6148
  38.2 5.3 %copy-start.4 = (s32[4,128]{1,0:T(4,128)S(1)}, s32[4,128]{1,0:T(4,128)}, u32[]{:S(2)}) copy-start(s32[4,128]{1,0:T(4,128)} %refs_7_.5) | copy-start | bytes 6148
  44.5 8.7 %collective-permute-start.5 = (f32[256,128]{1,0:T(8,128)S(1)}, f32[256,128]{1,0:T(8,128)S(1)}, u32[]{:S(2)}, u32[]{:S(2)}) collective-permute-start(f32[256,128]{1,0:T(8,128)S(1)} %shard_map.90.faces_ref.refs_0_), channel_id=1, source_target_pairs={{32,64},{64,32},{96,128},{128,96},{160,192},{192,160},{33,65},{65,... | collective-permute-start | bytes 393224 | tf_op jit(solution)/shard_map/ppermute | solution.py:399
  47.6 8.4 %collective-permute-start.6 = (f32[256,128]{1,0:T(8,128)S(1)}, f32[256,128]{1,0:T(8,128)S(1)}, u32[]{:S(2)}, u32[]{:S(2)}) collective-permute-start(f32[256,128]{1,0:T(8,128)S(1)} %shard_map.90.faces_ref.refs_0_), channel_id=1, source_target_pairs={{1,2},{2,1},{3,4},{4,3},{5,6},{6,5},{7,8},{8,7},{9,10},{10,9},{11,... | collective-permute-start | bytes 393224 | tf_op jit(solution)/shard_map/ppermute | solution.py:399
  51.1 5.1 %collective-permute-start.7 = (f32[256,128]{1,0:T(8,128)S(1)}, f32[256,128]{1,0:T(8,128)S(1)}, u32[]{:S(2)}, u32[]{:S(2)}) collective-permute-start(f32[256,128]{1,0:T(8,128)S(1)} %shard_map.90.faces_ref.refs_0_), channel_id=1, source_target_pairs={{0,32},{32,0},{64,96},{96,64},{128,160},{160,128},{192,224},{224,1... | collective-permute-start | bytes 393224 | tf_op jit(solution)/shard_map/ppermute | solution.py:399
  51.2 5.0 %collective-permute-start.8 = (f32[256,128]{1,0:T(8,128)S(1)}, f32[256,128]{1,0:T(8,128)S(1)}, u32[]{:S(2)}, u32[]{:S(2)}) collective-permute-start(f32[256,128]{1,0:T(8,128)S(1)} %shard_map.90.faces_ref.refs_0_), channel_id=1, source_target_pairs={{0,1},{1,0},{2,3},{3,2},{4,5},{5,4},{6,7},{7,6},{8,9},{9,8},{10,11... | collective-permute-start | bytes 393224 | tf_op jit(solution)/shard_map/ppermute | solution.py:399
  57.2 8.1 %collective-permute-start.10 = (f32[256,128]{1,0:T(8,128)S(1)}, f32[256,128]{1,0:T(8,128)S(1)}, u32[]{:S(2)}, u32[]{:S(2)}) collective-permute-start(f32[256,128]{1,0:T(8,128)S(1)} %shard_map.92.faces_ref.refs_0_), channel_id=1, source_target_pairs={{32,64},{64,32},{96,128},{128,96},{160,192},{192,160},{33,65},{65,... | collective-permute-start | bytes 393224 | tf_op jit(solution)/shard_map/ppermute | solution.py:399
  59.8 8.4 %collective-permute-start.11 = (f32[256,128]{1,0:T(8,128)S(1)}, f32[256,128]{1,0:T(8,128)S(1)}, u32[]{:S(2)}, u32[]{:S(2)}) collective-permute-start(f32[256,128]{1,0:T(8,128)S(1)} %shard_map.92.faces_ref.refs_0_), channel_id=1, source_target_pairs={{1,2},{2,1},{3,4},{4,3},{5,6},{6,5},{7,8},{8,7},{9,10},{10,9},{11,... | collective-permute-start | bytes 393224 | tf_op jit(solution)/shard_map/ppermute | solution.py:399
  62.9 5.3 %collective-permute-start.12 = (f32[256,128]{1,0:T(8,128)S(1)}, f32[256,128]{1,0:T(8,128)S(1)}, u32[]{:S(2)}, u32[]{:S(2)}) collective-permute-start(f32[256,128]{1,0:T(8,128)S(1)} %shard_map.92.faces_ref.refs_0_), channel_id=1, source_target_pairs={{0,32},{32,0},{64,96},{96,64},{128,160},{160,128},{192,224},{224,1... | collective-permute-start | bytes 393224 | tf_op jit(solution)/shard_map/ppermute | solution.py:399
  63.0 5.2 %collective-permute-start.9 = (f32[256,128]{1,0:T(8,128)S(1)}, f32[256,128]{1,0:T(8,128)S(1)}, u32[]{:S(2)}, u32[]{:S(2)}) collective-permute-start(f32[256,128]{1,0:T(8,128)S(1)} %shard_map.92.faces_ref.refs_0_), channel_id=1, source_target_pairs={{0,1},{1,0},{2,3},{3,2},{4,5},{5,4},{6,7},{7,6},{8,9},{9,8},{10,11... | collective-permute-start | bytes 393224 | tf_op jit(solution)/shard_map/ppermute | solution.py:399
